TPU v7x, 512 devices: a whole 4x4x16 slice. The times are simulated.
512 devices in a mesh: ctx: 128 (over z, x, core), kvh: 4 (over y).
Axes of the slice: x: 4, y: 4, z: 16, core: 2. Of those that a mesh axis runs over, the one named last changes fastest.
Arguments:
- queries: bfloat16 [32768, 4, 1024], P('ctx', 'kvh'), may hold values from -8 to 8
- keys: bfloat16 [32768, 1024], P('ctx', 'kvh'), may hold values from -8 to 8
- values: bfloat16 [32768, 1024], P('ctx', 'kvh'), may hold values from -6 to 6
- out_grad: bfloat16 [32768, 4, 1024], P('ctx', 'kvh'), may hold values from -6 to 6
- doc_lengths: int32 [64], replicated, may hold values from 1 to 768, 32768 in all
Outputs:
- query_grad: bfloat16 [32768, 4, 1024], P('ctx', 'kvh')
- key_grad: bfloat16 [32768, 1024], P('ctx', 'kvh')
- value_grad: bfloat16 [32768, 1024], P('ctx', 'kvh')
Inputs may be any that keep to these rules, and one draw needn't show every extreme that they name: `doc_lengths`: 64 documents in order that fill all 32768 positions; the longest has exactly 768 positions.
All inputs are finite; a program needn't handle non-finite values.
Results may differ from a plain program's by a relative error of at most 0.028.
Values may be sent and summed in bfloat16 or wider, within the bound.
No kernel may reach another device: no remote copies, remote signals or barrier semaphores. Data moves between devices by JAX's collectives and lax.ppermute only.
A program may use at most 64 MiB of HBM per device.

v0:
```python
import math

import jax
import jax.numpy as jnp
from jax import lax
from jax.sharding import PartitionSpec as P

HD = 128


def shifted(value, axis, by):
    length = lax.axis_size(axis)
    pairs = [(i, i + by) for i in range(length) if 0 <= i + by < length]
    return lax.ppermute(value, axis, pairs)


def doc_index(positions, ends):
    return jnp.sum((positions[:, None] >= ends[None, :]).astype(jnp.int32), axis=1)


def per_device(queries, keys, values, out_grad, doc_lengths):
    rows_here = queries.shape[0]
    head_size = HD
    scale = 1.0 / math.sqrt(head_size)
    ends = jnp.cumsum(doc_lengths)
    first_row = lax.axis_index("ctx") * rows_here
    key_here, value_here = (
        lax.all_gather(keys, "kvh", axis=1, tiled=True),
        lax.all_gather(values, "kvh", axis=1, tiled=True),
    )
    query_here, grad_here = (queries, out_grad)
    reps = query_here.shape[1]
    groups = key_here.shape[1] // head_size
    paired = jnp.stack([key_here, value_here])
    pieces = [paired]
    for level in range(3):
        pieces.append(shifted(pieces[-1], "ctx", 1))
    window = jnp.concatenate(pieces[::-1], axis=1)
    span = window.shape[1]
    query_pos = first_row + jnp.arange(rows_here, dtype=jnp.int32)
    key_pos = first_row - 3 * rows_here + jnp.arange(span, dtype=jnp.int32)
    query_seg = doc_index(query_pos, ends)
    key_seg = doc_index(key_pos, ends)
    allowed = (
        (query_seg[:, None] == key_seg[None, :])
        & (key_pos[None, :] <= query_pos[:, None])
        & (key_pos[None, :] >= 0)
    )
    head_queries = query_here.reshape(rows_here, reps, groups, head_size).transpose(2, 0, 1, 3)
    head_grads = grad_here.reshape(rows_here, reps, groups, head_size).transpose(2, 0, 1, 3)
    head_keys = window[0].reshape(span, groups, head_size).transpose(1, 0, 2)
    head_values = window[1].reshape(span, groups, head_size).transpose(1, 0, 2)

    def attend(operands):
        query_blk, grad_blk, key_blk, value_blk = operands
        scores = (
            jnp.einsum("qrd,kd->rqk", query_blk, key_blk, preferred_element_type=jnp.float32)
            * scale
        )
        scores = jnp.where(allowed[None], scores, -1e30)
        top = jnp.max(scores, axis=-1, keepdims=True)
        total = jnp.sum(
            jnp.where(allowed[None], jnp.exp(scores - top), 0.0), axis=-1, keepdims=True
        )
        log_total = top + jnp.log(total)
        weights = jnp.where(allowed[None], jnp.exp(scores - log_total), 0.0)
        weights_low = weights.astype(jnp.bfloat16)
        output = jnp.einsum(
            "rqk,kd->qrd", weights_low, value_blk, preferred_element_type=jnp.float32
        ).astype(jnp.bfloat16)
        delta = jnp.einsum("qrd,qrd->rq", grad_blk, output, preferred_element_type=jnp.float32)
        grad_weights = jnp.einsum(
            "qrd,kd->rqk", grad_blk, value_blk, preferred_element_type=jnp.float32
        )
        grad_scores = (weights * (grad_weights - delta[..., None])).astype(jnp.bfloat16)
        grad_query = (
            jnp.einsum("rqk,kd->qrd", grad_scores, key_blk, preferred_element_type=jnp.float32)
            * scale
        )
        grad_key = (
            jnp.einsum("rqk,qrd->kd", grad_scores, query_blk, preferred_element_type=jnp.float32)
            * scale
        )
        grad_value = jnp.einsum(
            "rqk,qrd->kd", weights_low, grad_blk, preferred_element_type=jnp.float32
        )
        return (grad_query, jnp.stack([grad_key, grad_value]))

    grad_query, grad_pair = lax.map(attend, (head_queries, head_grads, head_keys, head_values))
    grad_query = (
        grad_query.transpose(1, 2, 0, 3)
        .reshape(rows_here, reps, groups * head_size)
        .astype(jnp.bfloat16)
    )
    grad_pair = grad_pair.transpose(1, 2, 0, 3).reshape(2, span, groups * head_size)
    running = grad_pair[:, :rows_here]
    for level in range(1, 4):
        running = (
            shifted(running, "ctx", -1) + grad_pair[:, level * rows_here : (level + 1) * rows_here]
        )
    grad_pair = running
    grad_pair = lax.psum_scatter(grad_pair, "kvh", scatter_dimension=2, tiled=True)
    return (grad_query, grad_pair[0].astype(jnp.bfloat16), grad_pair[1].astype(jnp.bfloat16))


def solution(mesh):
    in_specs = (P("ctx", "kvh", None), P("ctx", "kvh"), P("ctx", "kvh"), P("ctx", "kvh", None), P())
    out_specs = (P("ctx", "kvh", None), P("ctx", "kvh"), P("ctx", "kvh"))
    return jax.shard_map(
        per_device, mesh=mesh, in_specs=in_specs, out_specs=out_specs, check_vma=False
    )
```

profile of v0, /device:TPU:1, one launch (start us, length us, event | category | flops | bytes accessed | tf_op | source)
XLA Modules:
  0.0 306.0 jit_solution(14351226921191410956)
XLA Ops:
  9.3 11.2 %all_gather.7 = bf16[256,1024]{0,1:T(8,128)(2,1)S(1)} all-gather(bf16[256,256]{0,1:T(8,128)(2,1)S(1)} %copy.23), channel_id=1, replica_groups=mesh['ctx'=128,'kvh'=4] {'kvh'}, dimensions={1}, use_global_device_ids=true | all-gather | bytes 655360 | tf_op jit(solution)/shard_map/all_gather | solution.py:29
  20.5 9.9 %all_gather.6 = bf16[256,1024]{0,1:T(8,128)(2,1)S(1)} all-gather(bf16[256,256]{0,1:T(8,128)(2,1)S(1)} %copy.22), channel_id=1, replica_groups=mesh['ctx'=128,'kvh'=4] {'kvh'}, dimensions={1}, use_global_device_ids=true | all-gather | bytes 655360 | tf_op jit(solution)/shard_map/all_gather | solution.py:28
  30.5 9.6 %collective-permute-start = (bf16[2,256,1024]{1,2,0:T(8,128)(2,1)S(1)}, bf16[2,256,1024]{1,2,0:T(8,128)(2,1)S(1)}, u32[]{:S(2)}, u32[]{:S(2)}) collective-permute-start(bf16[2,256,1024]{1,2,0:T(8,128)(2,1)S(1)} %pad_maximum_fusion), channel_id=1, source_target_pairs={{0,4},{4,8},{8,12},{12,16},{16,20},{20,24},{24,28},{28,32},{32,36}... | collective-permute-start | bytes 3145736 | tf_op jit(solution)/shard_map/ppermute | solution.py:14
  40.1 11.7 %collective-permute-done = bf16[2,256,1024]{1,2,0:T(8,128)(2,1)S(1)} collective-permute-done((bf16[2,256,1024]{1,2,0:T(8,128)(2,1)S(1)}, bf16[2,256,1024]{1,2,0:T(8,128)(2,1)S(1)}, u32[]{:S(2)}, u32[]{:S(2)}) %collective-permute-start) | collective-permute-done | bytes 1048608 | tf_op jit(solution)/shard_map/ppermute | solution.py:14
  51.8 4.4 %collective-permute-start.1 = (bf16[2,256,1024]{1,2,0:T(8,128)(2,1)S(1)}, bf16[2,256,1024]{1,2,0:T(8,128)(2,1)}, u32[]{:S(2)}, u32[]{:S(2)}) collective-permute-start(bf16[2,256,1024]{1,2,0:T(8,128)(2,1)S(1)} %collective-permute-done), channel_id=1, source_target_pairs={{0,4},{4,8},{8,12},{12,16},{16,20},{20,24},{24,28},{28,32},{32,36}... | collective-permute-start | bytes 3145736 | tf_op jit(solution)/shard_map/ppermute | solution.py:14
  56.2 11.7 %collective-permute-done.1 = bf16[2,256,1024]{1,2,0:T(8,128)(2,1)} collective-permute-done((bf16[2,256,1024]{1,2,0:T(8,128)(2,1)S(1)}, bf16[2,256,1024]{1,2,0:T(8,128)(2,1)}, u32[]{:S(2)}, u32[]{:S(2)}) %collective-permute-start.1) | collective-permute-done | bytes 1048608 | tf_op jit(solution)/shard_map/ppermute | solution.py:14
  67.9 4.5 %collective-permute-start.2 = (bf16[2,256,1024]{1,2,0:T(8,128)(2,1)}, bf16[2,256,1024]{1,2,0:T(8,128)(2,1)}, u32[]{:S(2)}, u32[]{:S(2)}) collective-permute-start(bf16[2,256,1024]{1,2,0:T(8,128)(2,1)} %collective-permute-done.1), channel_id=1, source_target_pairs={{0,4},{4,8},{8,12},{12,16},{16,20},{20,24},{24,28},{28,32},{32,36}... | collective-permute-start | bytes 3145736 | tf_op jit(solution)/shard_map/ppermute | solution.py:14
  75.1 9.3 %collective-permute-done.2 = bf16[2,256,1024]{1,2,0:T(8,128)(2,1)} collective-permute-done((bf16[2,256,1024]{1,2,0:T(8,128)(2,1)}, bf16[2,256,1024]{1,2,0:T(8,128)(2,1)}, u32[]{:S(2)}, u32[]{:S(2)}) %collective-permute-start.2) | collective-permute-done | bytes 1048608 | tf_op jit(solution)/shard_map/ppermute | solution.py:14
  84.5 1.8 maximum_maximum_fusion
  86.3 1.8 fusion.41
  88.1 61.7 %while.13 = (s32[]{:T(128)}, bf16[8,256,1,128]{1,3,2,0:T(8,128)(2,1)}, f32[8,2,1024,128]{3,2,1,0:T(8,128)}, bf16[8,1024,128]{1,2,0:T(8,128)(2,1)S(1)}, bf16[8,25...) while((s32[]{:T(128)}, ...), condition=%wide.region_6.7_spmd.clone, body=%wide.region_3.6_spmd.clone.sunk | while | flops 412941824 | bytes 12325017 | solution.py:89
  89.8 1.6 fusion.72
  105.3 1.6 fusion.72
  136.1 1.6 fusion.72
  143.8 1.6 fusion.72
  149.8 4.6 %copy_bitcast_fusion = f32[2,1024,1024]{2,1,0:T(8,128)S(1)} fusion(f32[8,2,1024,128]{3,2,1,0:T(8,128)} %get-tuple-element.47), kind=kLoop, calls=%fused_computation.50 | loop fusion | bytes 16777216 | tf_op jit(solution)/shard_map/reshape | solution.py:95
  154.6 1.9 collective-permute-start.3
  156.5 26.2 %collective-permute-done.3 = f32[2,256,1024]{2,1,0:T(8,128)S(1)} collective-permute-done((f32[2,256,1024]{2,1,0:T(8,128)S(1)}, f32[2,256,1024]{2,1,0:T(8,128)S(1)}, u32[]{:S(2)}, u32[]{:S(2)}) %collective-permute-start.3) | collective-permute-done | bytes 2097184 | tf_op jit(solution)/shard_map/ppermute | solution.py:14
  183.2 1.9 collective-permute-start.4
  185.1 25.4 %collective-permute-done.4 = f32[2,256,1024]{2,1,0:T(8,128)S(1)} collective-permute-done((f32[2,256,1024]{2,1,0:T(8,128)S(1)}, f32[2,256,1024]{2,1,0:T(8,128)S(1)}, u32[]{:S(2)}, u32[]{:S(2)}) %collective-permute-start.4) | collective-permute-done | bytes 2097184 | tf_op jit(solution)/shard_map/ppermute | solution.py:14
  211.0 2.1 collective-permute-start.5
  213.0 25.4 %collective-permute-done.5 = f32[2,256,1024]{2,1,0:T(8,128)S(1)} collective-permute-done((f32[2,256,1024]{2,1,0:T(8,128)S(1)}, f32[2,256,1024]{2,1,0:T(8,128)S(1)}, u32[]{:S(2)}, u32[]{:S(2)}) %collective-permute-start.5) | collective-permute-done | bytes 2097184 | tf_op jit(solution)/shard_map/ppermute | solution.py:14
  238.4 1.7 slice_add_fusion
  241.2 56.2 %reduce-scatter.2.cloned.1.call-done = f32[2,256,256]{2,1,0:T(8,128)} async-done(((f32[2,256,1024]{2,1,0:T(8,128)}), f32[2,256,256]{2,1,0:T(8,128)}) %reduce-scatter.2.cloned.1.call-update) | async-done | bytes 524304 | tf_op jit(solution)/shard_map/reduce_scatter | solution.py:102
  (127 shorter events, 63.5 us)
Async XLA Ops:
  7.2 66.3 %copy-start = (bf16[256,1,1024]{2,0,1:T(8,128)(2,1)S(1)}, bf16[256,1,1024]{2,0,1:T(8,128)(2,1)}, u32[]{:S(2)}) copy-start(bf16[256,1,1024]{2,0,1:T(8,128)(2,1)} %param.7) | copy-start | bytes 1572868
  7.2 290.2 %reduce-scatter.2.cloned.1.call-start = ((), (), s32[]{:S(2)}) async-start(), calls=%async_computation.1 | async-start | bytes 2621440 | tf_op jit(solution)/shard_map/reduce_scatter | solution.py:102
  30.5 21.3 %collective-permute-start = (bf16[2,256,1024]{1,2,0:T(8,128)(2,1)S(1)}, bf16[2,256,1024]{1,2,0:T(8,128)(2,1)S(1)}, u32[]{:S(2)}, u32[]{:S(2)}) collective-permute-start(bf16[2,256,1024]{1,2,0:T(8,128)(2,1)S(1)} %pad_maximum_fusion), channel_id=1, source_target_pairs={{0,4},{4,8},{8,12},{12,16},{16,20},{20,24},{24,28},{28,32},{32,36}... | collective-permute-start | bytes 3145736 | tf_op jit(solution)/shard_map/ppermute | solution.py:14
  51.8 16.1 %collective-permute-start.1 = (bf16[2,256,1024]{1,2,0:T(8,128)(2,1)S(1)}, bf16[2,256,1024]{1,2,0:T(8,128)(2,1)}, u32[]{:S(2)}, u32[]{:S(2)}) collective-permute-start(bf16[2,256,1024]{1,2,0:T(8,128)(2,1)S(1)} %collective-permute-done), channel_id=1, source_target_pairs={{0,4},{4,8},{8,12},{12,16},{16,20},{20,24},{24,28},{28,32},{32,36}... | collective-permute-start | bytes 3145736 | tf_op jit(solution)/shard_map/ppermute | solution.py:14
  67.9 16.5 %collective-permute-start.2 = (bf16[2,256,1024]{1,2,0:T(8,128)(2,1)}, bf16[2,256,1024]{1,2,0:T(8,128)(2,1)}, u32[]{:S(2)}, u32[]{:S(2)}) collective-permute-start(bf16[2,256,1024]{1,2,0:T(8,128)(2,1)} %collective-permute-done.1), channel_id=1, source_target_pairs={{0,4},{4,8},{8,12},{12,16},{16,20},{20,24},{24,28},{28,32},{32,36}... | collective-permute-start | bytes 3145736 | tf_op jit(solution)/shard_map/ppermute | solution.py:14
  154.6 28.1 %collective-permute-start.3 = (f32[2,256,1024]{2,1,0:T(8,128)S(1)}, f32[2,256,1024]{2,1,0:T(8,128)S(1)}, u32[]{:S(2)}, u32[]{:S(2)}) collective-permute-start(f32[2,256,1024]{2,1,0:T(8,128)S(1)} %slice.36), channel_id=1, source_target_pairs={{4,0},{8,4},{12,8},{16,12},{20,16},{24,20},{28,24},{32,28},{36,32}... | collective-permute-start | bytes 6291464 | tf_op jit(solution)/shard_map/ppermute | solution.py:14
  183.2 27.4 %collective-permute-start.4 = (f32[2,256,1024]{2,1,0:T(8,128)S(1)}, f32[2,256,1024]{2,1,0:T(8,128)S(1)}, u32[]{:S(2)}, u32[]{:S(2)}) collective-permute-start(f32[2,256,1024]{2,1,0:T(8,128)S(1)} %slice_add_fusion.2), channel_id=1, source_target_pairs={{4,0},{8,4},{12,8},{16,12},{20,16},{24,20},{28,24},{32,28},{36,32}... | collective-permute-start | bytes 6291464 | tf_op jit(solution)/shard_map/ppermute | solution.py:14
  210.9 29.3 %copy-start.1 = (bf16[8,256,1,128]{1,3,2,0:T(8,128)(2,1)S(1)}, bf16[8,256,1,128]{1,3,2,0:T(8,128)(2,1)}, u32[]{:S(2)}) copy-start(bf16[8,256,1,128]{1,3,2,0:T(8,128)(2,1)} %get-tuple-element.46) | copy-start | bytes 1572868
  211.0 27.5 %collective-permute-start.5 = (f32[2,256,1024]{2,1,0:T(8,128)S(1)}, f32[2,256,1024]{2,1,0:T(8,128)S(1)}, u32[]{:S(2)}, u32[]{:S(2)}) collective-permute-start(f32[2,256,1024]{2,1,0:T(8,128)S(1)} %slice_add_fusion.1), channel_id=1, source_target_pairs={{4,0},{8,4},{12,8},{16,12},{20,16},{24,20},{28,24},{32,28},{36,32}... | collective-permute-start | bytes 6291464 | tf_op jit(solution)/shard_map/ppermute | solution.py:14
Sparse Core Ops, SparseCore 0:
  240.3 57.0 reduce-scatter.1
where the time goes:
time: 307 us; the launch traced here: 306 us
  waiting for transfers between devices  166 us (54%)
  matrix products  44.2 us (14%)
  starting transfers between devices  24.4 us (8%)
  other arithmetic  21.3 us (7%)
  blocking collectives  21.1 us (7%)
  local copies, waits for them, and re-layouts  14.3 us (5%)
  between operations  14.2 us (5%)
    ppermute x6, waiting for transfers between devices, shifted(): return lax.ppermute(value, axis, pairs)  110 us
    reduce_scatter x1, waiting for transfers between devices, per_device(): lax.psum_scatter(grad_pair, 'kvh', scatter_dimension=2, tiled=True)  56.2 us
    ppermute x6, starting transfers between devices, shifted(): return lax.ppermute(value, axis, pairs)  24.3 us
    dot_general x8, matrix products, attend(): jnp.einsum('rqk,kd->qrd', weights_low, value_blk, preferred_element_type=...  12.9 us
    dot_general x8, matrix products, attend(): jnp.einsum('qrd,kd->rqk', grad_blk, value_blk, preferred_element_type=jnp...  12.5 us
    all_gather x1, blocking collectives, per_device(): lax.all_gather(values, 'kvh', axis=1, tiled=True)  11.2 us
    all_gather x1, blocking collectives, per_device(): lax.all_gather(keys, 'kvh', axis=1, tiled=True)  9.89 us
    dynamic_update_slice x8, other arithmetic, per_device(): lax.map(attend, (head_queries, head_grads, head_keys, head_values))  8.5 us
  transfers between devices with their start and end apart: 7, of which 7 were waited for; matrix products, arithmetic and copies ran while one was open for 1% of the time, Pallas kernels for 0%

commit v1 on v0

v1 whole, which is shorter than its diff:
```python
import math

import jax
import jax.numpy as jnp
from jax import lax
from jax.experimental import pallas as pl
from jax.experimental.pallas import tpu as pltpu
from jax.sharding import PartitionSpec as P

HD = 128
ROWS = 256
BACK = 3
SPAN = (BACK + 1) * ROWS
REPS = 4
HEADS = 2
SCALE = 1.0 / math.sqrt(HD)
LOG2E = 1.0 / math.log(2.0)

NT = (((1,), (1,)), ((), ()))
NN = (((1,), (0,)), ((), ()))
TN = (((0,), (0,)), ((), ()))


def dot(a, b, dims):
    return lax.dot_general(a, b, dims, preferred_element_type=jnp.float32)


def shifted(value, by):
    length = lax.axis_size("ctx")
    pairs = [(i, i + by) for i in range(length) if 0 <= i + by < length]
    return lax.ppermute(value, "ctx", pairs)


def pack_body(q_ref, g_ref, k_ref, v_ref, qg_ref, kv_ref):
    for y in range(REPS):
        cols = pl.ds(y * 256, 256)
        qg_ref[y, 0] = q_ref[0, :, cols]
        qg_ref[y, 1] = g_ref[0, :, cols]
    kv_ref[0] = k_ref[...]
    kv_ref[1] = v_ref[...]


def attend_body(
    len_ref, qg_ref, b0, b1, b2, b3, dq_ref, far0, far1, far2, own,
    s_ref, d_ref, w_ref, t_ref,
):
    blocks = (b0, b1, b2, b3)
    outs = (far0, far1, far2, own)
    docs = len_ref.shape[1]
    origin = lax.axis_index("ctx") * ROWS - BACK * ROWS
    at = lax.broadcasted_iota(jnp.int32, (docs, docs), 0)
    of = lax.broadcasted_iota(jnp.int32, (docs, docs), 1)
    ends = jnp.sum(jnp.where(of <= at, len_ref[...], 0), axis=1, keepdims=True)
    pos = origin + BACK * ROWS + lax.broadcasted_iota(jnp.int32, (docs, ROWS), 1)
    first = jnp.max(jnp.where(ends <= pos, ends, 0), axis=0, keepdims=True) - origin
    key_at = lax.broadcasted_iota(jnp.int32, (ROWS, ROWS), 0)
    row_at = lax.broadcasted_iota(jnp.int32, (ROWS, ROWS), 1)

    for h in range(HEADS):
        cols = pl.ds(h * HD, HD)
        for r in range(REPS):
            rows = pl.ds(r * ROWS, ROWS)
            query = qg_ref[r, 0, :, cols]
            grad = qg_ref[r, 1, :, cols]
            top = None
            for b in range(BACK + 1):
                s = dot(blocks[b][0, :, cols], query, NT)
                allowed = key_at >= first - b * ROWS
                if b == BACK:
                    allowed = allowed & (key_at <= row_at)
                s = jnp.where(allowed, s, -1e30)
                s_ref[r, pl.ds(b * ROWS, ROWS), :] = s
                part = jnp.max(s, axis=0, keepdims=True)
                top = part if top is None else jnp.maximum(top, part)
            total = jnp.zeros((1, ROWS), jnp.float32)
            inner = jnp.zeros((1, ROWS), jnp.float32)
            for b in range(BACK + 1):
                keys = pl.ds(b * ROWS, ROWS)
                p = jnp.exp2((s_ref[r, keys, :] - top) * (SCALE * LOG2E))
                d = dot(blocks[b][1, :, cols], grad, NT)
                total = total + jnp.sum(p, axis=0, keepdims=True)
                inner = inner + jnp.sum(p * d, axis=0, keepdims=True)
                s_ref[r, keys, :] = p
                d_ref[r, keys, :] = d
            norm = 1.0 / total
            delta = inner * norm
            for b in range(BACK + 1):
                keys = pl.ds(b * ROWS, ROWS)
                w = s_ref[r, keys, :] * norm
                w_ref[keys, rows] = w.astype(jnp.bfloat16)
                t_ref[keys, rows] = (w * (d_ref[r, keys, :] - delta)).astype(jnp.bfloat16)
            dq = None
            for b in range(BACK + 1):
                part = dot(blocks[b][0, :, cols], t_ref[pl.ds(b * ROWS, ROWS), rows], TN)
                dq = part if dq is None else dq + part
            dq_ref[r, :, cols] = (dq * SCALE).T.astype(jnp.bfloat16)
        queries = jnp.concatenate([qg_ref[r, 0, :, cols] for r in range(REPS)], axis=0)
        grads = jnp.concatenate([qg_ref[r, 1, :, cols] for r in range(REPS)], axis=0)
        for b in range(BACK + 1):
            keys = pl.ds(b * ROWS, ROWS)
            dk = dot(t_ref[keys, :], queries, NN) * SCALE
            dv = dot(w_ref[keys, :], grads, NN)
            outs[b][0, :, cols] = dk.astype(outs[b].dtype)
            outs[b][1, :, cols] = dv.astype(outs[b].dtype)


def finish_body(own, n1, n2, n3, dq_ref, k_ref, v_ref, q_ref):
    total = own[...] + (n1[...].astype(jnp.float32) + n2[...].astype(jnp.float32) + n3[...].astype(jnp.float32))
    k_ref[...] = total[0].astype(jnp.bfloat16)
    v_ref[...] = total[1].astype(jnp.bfloat16)
    for y in range(REPS):
        q_ref[0, :, pl.ds(y * 256, 256)] = dq_ref[y]


VM = pl.BlockSpec(memory_space=pltpu.VMEM)


def call(body, n_in, out_shape, scratch=(), flops=0, bytes_=1 << 20, vmem=48 << 20):
    return pl.pallas_call(
        body,
        out_shape=out_shape,
        in_specs=[VM] * n_in,
        out_specs=jax.tree.map(lambda _: VM, out_shape),
        scratch_shapes=list(scratch),
        compiler_params=pltpu.CompilerParams(vmem_limit_bytes=vmem),
        cost_estimate=pl.CostEstimate(flops=flops, bytes_accessed=bytes_, transcendentals=0),
    )


def shape(dims, dtype=jnp.bfloat16):
    return jax.ShapeDtypeStruct(dims, dtype)


def per_device(queries, keys, values, out_grad, doc_lengths):
    q = jnp.transpose(queries, (1, 0, 2))
    g = jnp.transpose(out_grad, (1, 0, 2))
    qg, kv = call(pack_body, 4, (shape((REPS, 2, ROWS, 256)), shape((2, ROWS, 256))))(q, g, keys, values)
    qg = lax.all_to_all(qg, "kvh", 0, 0, tiled=True)
    back = [shifted(kv, by) for by in (3, 2, 1)]
    block = (2, ROWS, 256)
    dq, far3, far2, far1, own = call(
        attend_body,
        6,
        (shape((REPS, ROWS, 256)), shape(block), shape(block), shape(block), shape(block, jnp.float32)),
        scratch=(
            pltpu.VMEM((REPS, SPAN, ROWS), jnp.float32),
            pltpu.VMEM((REPS, SPAN, ROWS), jnp.float32),
            pltpu.VMEM((SPAN, REPS * ROWS), jnp.bfloat16),
            pltpu.VMEM((SPAN, REPS * ROWS), jnp.bfloat16),
        ),
        flops=3 << 30,
    )(doc_lengths.reshape(1, -1), qg, *back, kv)
    n3, n2, n1 = shifted(far3, -3), shifted(far2, -2), shifted(far1, -1)
    dq = lax.all_to_all(dq, "kvh", 0, 0, tiled=True)
    dk, dv, dq = call(
        finish_body, 5, (shape((ROWS, 256)), shape((ROWS, 256)), shape((1, ROWS, 1024)))
    )(own, n1, n2, n3, dq)
    return jnp.transpose(dq, (1, 0, 2)), dk, dv


def solution(mesh):
    in_specs = (P("ctx", "kvh", None), P("ctx", "kvh"), P("ctx", "kvh"), P("ctx", "kvh", None), P())
    out_specs = (P("ctx", "kvh", None), P("ctx", "kvh"), P("ctx", "kvh"))
    return jax.shard_map(
        per_device, mesh=mesh, in_specs=in_specs, out_specs=out_specs, check_vma=False
    )
```

time: 307 us -> 70.7 us (0.23)
  the two profiles are of different devices: /device:TPU:1 before, /device:TPU:205 now
where the time goes in v1:
time: 70.7 us; the launch traced here: 70.2 us
  starting transfers between devices  29.8 us (42%)
  waiting for transfers between devices  24.2 us (34%)
  Pallas kernels  11.6 us (16%)
  local copies, waits for them, and re-layouts  3.89 us (6%)
  between operations  0.71 us (1%)
    ppermute x6, waiting for transfers between devices, shifted(): return lax.ppermute(value, 'ctx', pairs)  24.2 us
    ppermute x6, starting transfers between devices, shifted(): return lax.ppermute(value, 'ctx', pairs)  21.2 us
    pallas_call x1, Pallas kernels, per_device(): call(attend_body, 6, (shape((REPS, ROWS, 256)), shape(block), shape(block...  9.53 us
    all_to_all x1, starting transfers between devices, per_device(): qg = lax.all_to_all(qg, 'kvh', 0, 0, tiled=True)  4.35 us
    all_to_all x1, starting transfers between devices, per_device(): dq = lax.all_to_all(dq, 'kvh', 0, 0, tiled=True)  4.24 us
    unnamed x10, local copies, waits for them, and re-layouts  3.89 us
  transfers between devices with their start and end apart: 8, of which 4 were waited for; matrix products, arithmetic and copies ran while one was open for 0% of the time, Pallas kernels for 0%

profile of v1, /device:TPU:205, one launch (start us, length us, event | category | flops | bytes accessed | tf_op | source)
XLA Modules:
  0.0 70.2 jit_solution(936403362901117625)
XLA Ops:
  0.6 0.0 copy-start
  0.6 1.0 %copy-done = bf16[256,1,1024]{2,0,1:T(8,128)(2,1)S(1)} copy-done((bf16[256,1,1024]{2,0,1:T(8,128)(2,1)S(1)}, bf16[256,1,1024]{2,0,1:T(8,128)(2,1)}, u32[]{:S(2)}) %copy-start) | copy-done | bytes 524312
  1.7 1.0 %copy-done.1 = bf16[256,1,1024]{2,0,1:T(8,128)(2,1)S(1)} copy-done((bf16[256,1,1024]{2,0,1:T(8,128)(2,1)S(1)}, bf16[256,1,1024]{2,0,1:T(8,128)(2,1)}, u32[]{:S(2)}) %copy-start.1) | copy-done | bytes 524312
  2.7 0.9 %copy-done.2 = bf16[256,256]{1,0:T(8,128)(2,1)S(1)} copy-done((bf16[256,256]{1,0:T(8,128)(2,1)S(1)}, bf16[256,256]{1,0:T(8,128)(2,1)}, u32[]{:S(2)}) %copy-start.2) | copy-done | bytes 131096
  3.6 0.9 %copy-done.3 = bf16[256,256]{1,0:T(8,128)(2,1)S(1)} copy-done((bf16[256,256]{1,0:T(8,128)(2,1)S(1)}, bf16[256,256]{1,0:T(8,128)(2,1)}, u32[]{:S(2)}) %copy-start.3) | copy-done | bytes 131096
  4.5 1.1 %shard_map.76 = (bf16[4,2,256,256]{3,2,1,0:T(8,128)(2,1)}, bf16[2,256,256]{2,1,0:T(8,128)(2,1)S(1)}) custom-call(bf16[1,256,1024]{2,1,0:T(8,128)(2,1)S(1)} %bitcast.4, bf16[1,256,1024]{2,1,0:T(8,128)(2,1)S(1)} %bitcast.5, bf16[256,256]{1,0:T(8,128)(2,1)S(1)} %copy-done.2, bf16[256,256]{1,0:T(8,128)(2,1)S(1)} %copy-done.3), custom_call_target="tpu_custom_call" | custom-call | bytes 1048576 | tf_op jit(solution)/shard_map/pallas_call | solution.py:137
  5.6 4.3 %all-to-all-start = ((bf16[4,2,256,256]{3,2,1,0:T(8,128)(2,1)}), bf16[4,2,256,256]{3,2,1,0:T(8,128)(2,1)S(1)}, u32[]{:S(2)}, u32[]{:S(2)}) async-start(bf16[4,2,256,256]{3,2,1,0:T(8,128)(2,1)} %get-tuple-element.13), calls=%async_computation | async-start | bytes 2097152 | tf_op jit(solution)/shard_map/all_to_all | solution.py:138
  9.9 4.1 %collective-permute-start.2 = (bf16[2,256,256]{2,1,0:T(8,128)(2,1)S(1)}, bf16[2,256,256]{2,1,0:T(8,128)(2,1)S(1)}, u32[]{:S(2)}, u32[]{:S(2)}) collective-permute-start(bf16[2,256,256]{2,1,0:T(8,128)(2,1)S(1)} %get-tuple-element.14.b3), channel_id=1, source_target_pairs={{0,4},{4,8},{8,12},{12,16},{16,20},{20,24},{24,28},{28,32},{32,36}... | collective-permute-start | bytes 786440 | tf_op jit(solution)/shard_map/ppermute | solution.py:31
  14.0 3.5 %collective-permute-start.1 = (bf16[2,256,256]{2,1,0:T(8,128)(2,1)S(1)}, bf16[2,256,256]{2,1,0:T(8,128)(2,1)S(1)}, u32[]{:S(2)}, u32[]{:S(2)}) collective-permute-start(bf16[2,256,256]{2,1,0:T(8,128)(2,1)S(1)} %get-tuple-element.14.b3), channel_id=1, source_target_pairs={{0,8},{4,12},{8,16},{12,20},{16,24},{20,28},{24,32},{28,36},{32,40... | collective-permute-start | bytes 786440 | tf_op jit(solution)/shard_map/ppermute | solution.py:31
  17.5 2.5 %collective-permute-start = (bf16[2,256,256]{2,1,0:T(8,128)(2,1)S(1)}, bf16[2,256,256]{2,1,0:T(8,128)(2,1)S(1)}, u32[]{:S(2)}, u32[]{:S(2)}) collective-permute-start(bf16[2,256,256]{2,1,0:T(8,128)(2,1)S(1)} %get-tuple-element.14.b3), channel_id=1, source_target_pairs={{0,12},{4,16},{8,20},{12,24},{16,28},{20,32},{24,36},{28,40},{32,4... | collective-permute-start | bytes 786440 | tf_op jit(solution)/shard_map/ppermute | solution.py:31
  20.0 0.0 collective-permute-done.2.b2
  20.0 6.4 %collective-permute-done.1.b1 = bf16[2,256,256]{2,1,0:T(8,128)(2,1)S(1)} collective-permute-done((bf16[2,256,256]{2,1,0:T(8,128)(2,1)S(1)}, bf16[2,256,256]{2,1,0:T(8,128)(2,1)S(1)}, u32[]{:S(2)}, u32[]{:S(2)}) %collective-permute-start.1) | collective-permute-done | bytes 262176 | tf_op jit(solution)/shard_map/ppermute | solution.py:31
  26.4 3.1 %collective-permute-done.b0 = bf16[2,256,256]{2,1,0:T(8,128)(2,1)S(1)} collective-permute-done((bf16[2,256,256]{2,1,0:T(8,128)(2,1)S(1)}, bf16[2,256,256]{2,1,0:T(8,128)(2,1)S(1)}, u32[]{:S(2)}, u32[]{:S(2)}) %collective-permute-start) | collective-permute-done | bytes 262176 | tf_op jit(solution)/shard_map/ppermute | solution.py:31
  29.5 0.0 all-to-all-done.qg_ref
  29.5 9.5 %shard_map.77 = (bf16[4,256,256]{2,1,0:T(8,128)(2,1)}, bf16[2,256,256]{2,1,0:T(8,128)(2,1)S(1)}, bf16[2,256,256]{2,1,0:T(8,128)(2,1)S(1)}, bf16[2,256,256]{2,1,0:T(8,128)(2,1)S(1)}, f32[2,256,256]{2,1,0:T(8,128)S(1)}) custom-call(s32[1,64]{1,0:T(1,128)S(1)} %bitcast.6, bf16[4,2,256,256]{3,2,1,0:T(8,128)(2,1)S(1)} %all-to-all-done.qg_ref, ...), custom_call_target="tpu_custom_call" | custom-call | flops 3221225472 | bytes 1048576 | tf_op jit(solution)/shard_map/pallas_call | solution.py:141
  39.1 4.2 %all-to-all-start.1 = ((bf16[4,256,256]{2,1,0:T(8,128)(2,1)}), bf16[4,256,256]{2,1,0:T(8,128)(2,1)S(1)}, u32[]{:S(2)}, u32[]{:S(2)}) async-start(bf16[4,256,256]{2,1,0:T(8,128)(2,1)} %get-tuple-element.19), calls=%async_computation.1 | async-start | bytes 1048576 | tf_op jit(solution)/shard_map/all_to_all | solution.py:154
  43.3 3.2 %collective-permute-start.3 = (bf16[2,256,256]{2,1,0:T(8,128)(2,1)S(1)}, bf16[2,256,256]{2,1,0:T(8,128)(2,1)S(1)}, u32[]{:S(2)}, u32[]{:S(2)}) collective-permute-start(bf16[2,256,256]{2,1,0:T(8,128)(2,1)S(1)} %get-tuple-element.16), channel_id=1, source_target_pairs={{4,0},{8,4},{12,8},{16,12},{20,16},{24,20},{28,24},{32,28},{36,32}... | collective-permute-start | bytes 786440 | tf_op jit(solution)/shard_map/ppermute | solution.py:31
  46.5 6.1 %collective-permute-start.4 = (bf16[2,256,256]{2,1,0:T(8,128)(2,1)S(1)}, bf16[2,256,256]{2,1,0:T(8,128)(2,1)S(1)}, u32[]{:S(2)}, u32[]{:S(2)}) collective-permute-start(bf16[2,256,256]{2,1,0:T(8,128)(2,1)S(1)} %get-tuple-element.17), channel_id=1, source_target_pairs={{8,0},{12,4},{16,8},{20,12},{24,16},{28,20},{32,24},{36,28},{40,32... | collective-permute-start | bytes 786440 | tf_op jit(solution)/shard_map/ppermute | solution.py:31
  52.6 1.9 %collective-permute-start.5 = (bf16[2,256,256]{2,1,0:T(8,128)(2,1)S(1)}, bf16[2,256,256]{2,1,0:T(8,128)(2,1)S(1)}, u32[]{:S(2)}, u32[]{:S(2)}) collective-permute-start(bf16[2,256,256]{2,1,0:T(8,128)(2,1)S(1)} %get-tuple-element.18), channel_id=1, source_target_pairs={{12,0},{16,4},{20,8},{24,12},{28,16},{32,20},{36,24},{40,28},{44,3... | collective-permute-start | bytes 786440 | tf_op jit(solution)/shard_map/ppermute | solution.py:31
  54.5 0.0 collective-permute-done.3.n1
  54.5 3.8 %collective-permute-done.4.n2 = bf16[2,256,256]{2,1,0:T(8,128)(2,1)S(1)} collective-permute-done((bf16[2,256,256]{2,1,0:T(8,128)(2,1)S(1)}, bf16[2,256,256]{2,1,0:T(8,128)(2,1)S(1)}, u32[]{:S(2)}, u32[]{:S(2)}) %collective-permute-start.4) | collective-permute-done | bytes 262176 | tf_op jit(solution)/shard_map/ppermute | solution.py:31
  58.3 11.0 %collective-permute-done.5.n3 = bf16[2,256,256]{2,1,0:T(8,128)(2,1)S(1)} collective-permute-done((bf16[2,256,256]{2,1,0:T(8,128)(2,1)S(1)}, bf16[2,256,256]{2,1,0:T(8,128)(2,1)S(1)}, u32[]{:S(2)}, u32[]{:S(2)}) %collective-permute-start.5) | collective-permute-done | bytes 262176 | tf_op jit(solution)/shard_map/ppermute | solution.py:31
  69.2 0.0 all-to-all-done.1.dq_ref
  69.2 1.0 %shard_map.78 = (bf16[256,256]{1,0:T(8,128)(2,1)}, bf16[256,256]{1,0:T(8,128)(2,1)}, bf16[1,256,1024]{2,1,0:T(8,128)(2,1)}) custom-call(f32[2,256,256]{2,1,0:T(8,128)S(1)} %get-tuple-element.15.own, bf16[2,256,256]{2,1,0:T(8,128)(2,1)S(1)} %collective-permute-done.3.n1, bf16[2,256,256]{2,1,0:T(8,128)(2,1)S(1)} %collective-permute-done.4.n2, ...), custom_call_target="tpu_custom_call" | custom-call | bytes 1048576 | tf_op jit(solution)/shard_map/pallas_call | solution.py:155
  (5 shorter events, 0.0 us)
Async XLA Ops:
  0.6 1.0 %copy-start = (bf16[256,1,1024]{2,0,1:T(8,128)(2,1)S(1)}, bf16[256,1,1024]{2,0,1:T(8,128)(2,1)}, u32[]{:S(2)}) copy-start(bf16[256,1,1024]{2,0,1:T(8,128)(2,1)} %param.5) | copy-start | bytes 1572868
  1.7 1.0 %copy-start.1 = (bf16[256,1,1024]{2,0,1:T(8,128)(2,1)S(1)}, bf16[256,1,1024]{2,0,1:T(8,128)(2,1)}, u32[]{:S(2)}) copy-start(bf16[256,1,1024]{2,0,1:T(8,128)(2,1)} %param.8) | copy-start | bytes 1572868
  2.7 0.9 %copy-start.2 = (bf16[256,256]{1,0:T(8,128)(2,1)S(1)}, bf16[256,256]{1,0:T(8,128)(2,1)}, u32[]{:S(2)}) copy-start(bf16[256,256]{1,0:T(8,128)(2,1)} %k_ref.1) | copy-start | bytes 393220
  3.6 0.9 %copy-start.3 = (bf16[256,256]{1,0:T(8,128)(2,1)S(1)}, bf16[256,256]{1,0:T(8,128)(2,1)}, u32[]{:S(2)}) copy-start(bf16[256,256]{1,0:T(8,128)(2,1)} %v_ref.1) | copy-start | bytes 393220
  5.6 23.9 %all-to-all-start = ((bf16[4,2,256,256]{3,2,1,0:T(8,128)(2,1)}), bf16[4,2,256,256]{3,2,1,0:T(8,128)(2,1)S(1)}, u32[]{:S(2)}, u32[]{:S(2)}) async-start(bf16[4,2,256,256]{3,2,1,0:T(8,128)(2,1)} %get-tuple-element.13), calls=%async_computation | async-start | bytes 2097152 | tf_op jit(solution)/shard_map/all_to_all | solution.py:138
  9.9 19.6 %copy-start.4 = (s32[64]{0:T(128)S(1)}, s32[64]{0:T(128)}, u32[]{:S(2)}) copy-start(s32[64]{0:T(128)} %param.9) | copy-start | bytes 772
  9.9 10.1 %collective-permute-start.2 = (bf16[2,256,256]{2,1,0:T(8,128)(2,1)S(1)}, bf16[2,256,256]{2,1,0:T(8,128)(2,1)S(1)}, u32[]{:S(2)}, u32[]{:S(2)}) collective-permute-start(bf16[2,256,256]{2,1,0:T(8,128)(2,1)S(1)} %get-tuple-element.14.b3), channel_id=1, source_target_pairs={{0,4},{4,8},{8,12},{12,16},{16,20},{20,24},{24,28},{28,32},{32,36}... | collective-permute-start | bytes 786440 | tf_op jit(solution)/shard_map/ppermute | solution.py:31
  14.0 12.4 %collective-permute-start.1 = (bf16[2,256,256]{2,1,0:T(8,128)(2,1)S(1)}, bf16[2,256,256]{2,1,0:T(8,128)(2,1)S(1)}, u32[]{:S(2)}, u32[]{:S(2)}) collective-permute-start(bf16[2,256,256]{2,1,0:T(8,128)(2,1)S(1)} %get-tuple-element.14.b3), channel_id=1, source_target_pairs={{0,8},{4,12},{8,16},{12,20},{16,24},{20,28},{24,32},{28,36},{32,40... | collective-permute-start | bytes 786440 | tf_op jit(solution)/shard_map/ppermute | solution.py:31
  17.5 12.0 %collective-permute-start = (bf16[2,256,256]{2,1,0:T(8,128)(2,1)S(1)}, bf16[2,256,256]{2,1,0:T(8,128)(2,1)S(1)}, u32[]{:S(2)}, u32[]{:S(2)}) collective-permute-start(bf16[2,256,256]{2,1,0:T(8,128)(2,1)S(1)} %get-tuple-element.14.b3), channel_id=1, source_target_pairs={{0,12},{4,16},{8,20},{12,24},{16,28},{20,32},{24,36},{28,40},{32,4... | collective-permute-start | bytes 786440 | tf_op jit(solution)/shard_map/ppermute | solution.py:31
  39.1 30.2 %all-to-all-start.1 = ((bf16[4,256,256]{2,1,0:T(8,128)(2,1)}), bf16[4,256,256]{2,1,0:T(8,128)(2,1)S(1)}, u32[]{:S(2)}, u32[]{:S(2)}) async-start(bf16[4,256,256]{2,1,0:T(8,128)(2,1)} %get-tuple-element.19), calls=%async_computation.1 | async-start | bytes 1048576 | tf_op jit(solution)/shard_map/all_to_all | solution.py:154
  43.3 11.2 %collective-permute-start.3 = (bf16[2,256,256]{2,1,0:T(8,128)(2,1)S(1)}, bf16[2,256,256]{2,1,0:T(8,128)(2,1)S(1)}, u32[]{:S(2)}, u32[]{:S(2)}) collective-permute-start(bf16[2,256,256]{2,1,0:T(8,128)(2,1)S(1)} %get-tuple-element.16), channel_id=1, source_target_pairs={{4,0},{8,4},{12,8},{16,12},{20,16},{24,20},{28,24},{32,28},{36,32}... | collective-permute-start | bytes 786440 | tf_op jit(solution)/shard_map/ppermute | solution.py:31
  46.5 11.8 %collective-permute-start.4 = (bf16[2,256,256]{2,1,0:T(8,128)(2,1)S(1)}, bf16[2,256,256]{2,1,0:T(8,128)(2,1)S(1)}, u32[]{:S(2)}, u32[]{:S(2)}) collective-permute-start(bf16[2,256,256]{2,1,0:T(8,128)(2,1)S(1)} %get-tuple-element.17), channel_id=1, source_target_pairs={{8,0},{12,4},{16,8},{20,12},{24,16},{28,20},{32,24},{36,28},{40,32... | collective-permute-start | bytes 786440 | tf_op jit(solution)/shard_map/ppermute | solution.py:31
  52.6 16.7 %collective-permute-start.5 = (bf16[2,256,256]{2,1,0:T(8,128)(2,1)S(1)}, bf16[2,256,256]{2,1,0:T(8,128)(2,1)S(1)}, u32[]{:S(2)}, u32[]{:S(2)}) collective-permute-start(bf16[2,256,256]{2,1,0:T(8,128)(2,1)S(1)} %get-tuple-element.18), channel_id=1, source_target_pairs={{12,0},{16,4},{20,8},{24,12},{28,16},{32,20},{36,24},{40,28},{44,3... | collective-permute-start | bytes 786440 | tf_op jit(solution)/shard_map/ppermute | solution.py:31

commit v2 on v1

v2 whole, which is shorter than its diff:
```python
import math

import jax
import jax.numpy as jnp
from jax import lax
from jax.experimental import pallas as pl
from jax.experimental.pallas import tpu as pltpu
from jax.sharding import PartitionSpec as P

HD = 128
ROWS = 256
BACK = 3
REPS = 4
HEADS = 2
SCALE = 1.0 / math.sqrt(HD)
RATE = SCALE / math.log(2.0)
NEAR = BACK * ROWS
UNITS = [(h, r) for h in range(HEADS) for r in range(REPS)]

NT = (((1,), (1,)), ((), ()))
NN = (((1,), (0,)), ((), ()))
TN = (((0,), (0,)), ((), ()))


def dot(a, b, dims):
    return lax.dot_general(a, b, dims, preferred_element_type=jnp.float32)


def sent(value, even, odd):
    length = lax.axis_size("ctx")
    moves = [(i, i + (odd if i % 2 else even)) for i in range(length)]
    return lax.ppermute(value, "ctx", [(i, j) for i, j in moves if 0 <= j < length])


def cols(h):
    return pl.ds(h * HD, HD)


def block_rows(b):
    return pl.ds(b * ROWS, ROWS)


def pack_body(len_ref, k_ref, v_ref, q_ref, g_ref, kv_ref, qg_ref, first_ref, len_buf, kv_buf, qg_buf, len_sem, sems):
    moves = [
        (ref.at[0, :, pl.ds(y * 256, 256)], qg_buf.at[y, a], qg_ref.at[y, a])
        for y in range(REPS)
        for a, ref in enumerate((q_ref, g_ref))
    ] + [(ref, kv_buf.at[a], kv_ref.at[a]) for a, ref in enumerate((k_ref, v_ref))]
    ins = [pltpu.make_async_copy(a, b, sems.at[0, n]) for n, (a, b, _) in enumerate(moves)]
    outs = [pltpu.make_async_copy(b, c, sems.at[1, n]) for n, (_, b, c) in enumerate(moves)]
    lens = pltpu.make_async_copy(len_ref, len_buf, len_sem)
    lens.start()
    for copy in ins:
        copy.start()
    lens.wait()
    first_ref[...] = doc_first(len_buf, lax.axis_index("ctx") * ROWS)
    for copy, after in zip(ins, outs):
        copy.wait()
        after.start()
    for copy in outs:
        copy.wait()


def doc_first(len_ref, origin):
    docs = len_ref.shape[1]
    at = lax.broadcasted_iota(jnp.int32, (docs, docs), 0)
    of = lax.broadcasted_iota(jnp.int32, (docs, docs), 1)
    ends = jnp.sum(jnp.where(of <= at, len_ref[...], 0), axis=1, keepdims=True)
    pos = origin + lax.broadcasted_iota(jnp.int32, (docs, ROWS), 1)
    return jnp.max(jnp.where(ends <= pos, ends, 0), axis=0, keepdims=True) - origin


def passed_back():
    odd = lax.rem(lax.axis_index("ctx"), 2)
    return 3 - 2 * odd, 1 + 2 * odd


def score(first, back, key, query):
    key_at = lax.broadcasted_iota(jnp.int32, (ROWS, ROWS), 0)
    allowed = key_at >= first + back * ROWS
    if isinstance(back, int) and back == 0:
        allowed = allowed & (key_at <= lax.broadcasted_iota(jnp.int32, (ROWS, ROWS), 1))
    return jnp.where(allowed, dot(key, query, NT), -1e30)


def near_body(first_ref, qg_ref, *refs):
    count = len(refs) - 5
    blocks = refs[:count]
    p_ref, d_ref, top_ref, total_ref, inner_ref = refs[count:]
    first = first_ref[...]
    backs = (2, passed_back()[0], 0)
    tops, totals, inners = {}, {}, {}

    def scores(u, n):
        h, r = UNITS[u]
        s = score(first, backs[n], blocks[n][0, :, cols(h)], qg_ref[r, 0, :, cols(h)])
        p_ref[u, block_rows(n), :] = s
        part = jnp.max(s, axis=0, keepdims=True)
        tops[u] = part if n == 0 else jnp.maximum(tops[u], part)

    def weigh(u, n):
        h, r = UNITS[u]
        p = jnp.exp2((p_ref[u, block_rows(n), :] - tops[u]) * RATE)
        d = dot(blocks[n][1, :, cols(h)], qg_ref[r, 1, :, cols(h)], NT)
        p_ref[u, block_rows(n), :] = p
        d_ref[u, block_rows(n), :] = d
        total, inner = jnp.sum(p, axis=0, keepdims=True), jnp.sum(p * d, axis=0, keepdims=True)
        totals[u] = total if n == 0 else totals[u] + total
        inners[u] = inner if n == 0 else inners[u] + inner
        if n == count - 1:
            top_ref[pl.ds(u, 1), :] = tops[u]
            total_ref[pl.ds(u, 1), :] = totals[u]
            inner_ref[pl.ds(u, 1), :] = inners[u]

    for step in range(len(UNITS) + 1):
        for n in range(count):
            if step < len(UNITS):
                scores(step, n)
            if step >= 1:
                weigh(step - 1, n)


def far_body(
    first_ref, top_ref, total_ref, inner_ref, p_ref, d_ref, qg_ref, *refs
):
    blocks = refs[:BACK + 1]
    outs = refs[BACK + 1:2 * BACK + 1]
    own_ref, dq_ref, s0_ref, d0_ref, w_ref, t_ref = refs[2 * BACK + 1:]
    near = p_ref.shape[1] // ROWS
    first = first_ref[...]
    backs = (passed_back()[1],)
    outs = outs[:near - 1] + (own_ref,) + outs[near - 1:]
    stats, norms = {}, {}

    def scores(u):
        h, r = UNITS[u]
        for b in range(near, BACK + 1):
            s = score(first, backs[b - near], blocks[b][0, :, cols(h)], qg_ref[r, 0, :, cols(h)])
            s0_ref[u, block_rows(b - near), :] = s
            top = jnp.max(s, axis=0, keepdims=True)
            stats[u] = top if b == near else jnp.maximum(top, stats[u])

    def weigh(u):
        h, r = UNITS[u]
        top = stats[u]
        far_total = far_inner = 0.0
        for b in range(near, BACK + 1):
            rows = block_rows(b - near)
            p = jnp.exp2((s0_ref[u, rows, :] - top) * RATE)
            d = dot(blocks[b][1, :, cols(h)], qg_ref[r, 1, :, cols(h)], NT)
            s0_ref[u, rows, :] = p
            d0_ref[u, rows, :] = d
            far_total = far_total + jnp.sum(p, axis=0, keepdims=True)
            far_inner = far_inner + jnp.sum(p * d, axis=0, keepdims=True)
        row = pl.ds(u, 1)
        whole = jnp.maximum(top, top_ref[row, :])
        far_part, near_part = jnp.exp2((top - whole) * RATE), jnp.exp2((top_ref[row, :] - whole) * RATE)
        total = near_part * total_ref[row, :] + far_part * far_total
        inner = near_part * inner_ref[row, :] + far_part * far_inner
        inverse = 1.0 / total
        norms[u] = (far_part * inverse, near_part * inverse, inner * inverse)

    def settle(u, b):
        h, r = UNITS[u]
        far_norm, near_norm, delta = norms[u]
        at = pl.ds(r * ROWS, ROWS)
        if b >= near:
            w, d = s0_ref[u, block_rows(b - near), :] * far_norm, d0_ref[u, block_rows(b - near), :]
        else:
            w, d = p_ref[u, block_rows(b), :] * near_norm, d_ref[u, block_rows(b), :]
        low, t = w.astype(jnp.bfloat16), (w * (d - delta)).astype(jnp.bfloat16)
        t_ref[h, block_rows(b), at] = t
        w_ref[h, block_rows(b), at] = low

    def query_grad(u):
        h, r = UNITS[u]
        keys = jnp.concatenate([block[0, :, cols(h)] for block in blocks], axis=0)
        dq = dot(keys, t_ref[h, :, pl.ds(r * ROWS, ROWS)], TN) * SCALE
        dq_ref[r, :, cols(h)] = dq.T.astype(jnp.bfloat16)

    def gather(h, b):
        queries = jnp.concatenate([qg_ref[r, 0, :, cols(h)] for r in range(REPS)], axis=0)
        grads = jnp.concatenate([qg_ref[r, 1, :, cols(h)] for r in range(REPS)], axis=0)
        dk = dot(t_ref[h, block_rows(b), :], queries, NN) * SCALE
        dv = dot(w_ref[h, block_rows(b), :], grads, NN)
        outs[b][0, :, cols(h)] = dk.astype(outs[b].dtype)
        outs[b][1, :, cols(h)] = dv.astype(outs[b].dtype)

    for step in range(len(UNITS) + 3):
        if step < len(UNITS):
            scores(step)
        if 0 <= step - 1 < len(UNITS):
            weigh(step - 1)
        if 0 <= step - 2 < len(UNITS):
            for b in range(BACK + 1):
                settle(step - 2, b)
        if 0 <= step - 3 < len(UNITS):
            query_grad(step - 3)
        if 0 <= step - 6 <= BACK:
            gather(0, step - 6)
    for b in range(BACK + 1):
        gather(1, b)


def add_body(a_ref, b_ref, c_ref):
    c_ref[...] = (a_ref[...].astype(jnp.float32) + b_ref[...].astype(jnp.float32)).astype(jnp.bfloat16)


def finish_body(own, n1, n2, dq_ref, k_ref, v_ref, q_ref):
    total = own[...] + (n1[...].astype(jnp.float32) + n2[...].astype(jnp.float32))
    k_ref[...] = total[0].astype(jnp.bfloat16)
    v_ref[...] = total[1].astype(jnp.bfloat16)
    for y in range(REPS):
        q_ref[0, :, pl.ds(y * 256, 256)] = dq_ref[y]


VM = pl.BlockSpec(memory_space=pltpu.VMEM)
ANY = pl.BlockSpec(memory_space=pl.ANY)


def call(body, n_in, out_shape, scratch=(), flops=0, bytes_=1 << 20, vmem=16 << 20, spec=VM, ospec=None):
    return pl.pallas_call(
        body,
        out_shape=out_shape,
        in_specs=[spec] * n_in,
        out_specs=ospec or jax.tree.map(lambda _: spec, out_shape),
        scratch_shapes=list(scratch),
        compiler_params=pltpu.CompilerParams(vmem_limit_bytes=vmem),
        cost_estimate=pl.CostEstimate(flops=flops, bytes_accessed=bytes_, transcendentals=0),
    )


def shape(dims, dtype=jnp.bfloat16):
    return jax.ShapeDtypeStruct(dims, dtype)


def per_device(queries, keys, values, out_grad, doc_lengths):
    q = jnp.transpose(queries, (1, 0, 2))
    g = jnp.transpose(out_grad, (1, 0, 2))
    block = (2, ROWS, 256)
    kv, qg, first = call(
        pack_body,
        5,
        (shape(block), shape((REPS, 2, ROWS, 256)), shape((1, ROWS), jnp.int32)),
        scratch=[
            pltpu.VMEM((1, doc_lengths.shape[0]), jnp.int32),
            pltpu.VMEM(block, jnp.bfloat16),
            pltpu.VMEM((REPS, 2, ROWS, 256), jnp.bfloat16),
            pltpu.SemaphoreType.DMA,
            pltpu.SemaphoreType.DMA((2, 10)),
        ],
        spec=ANY,
        ospec=(ANY, ANY, VM),
        vmem=4 << 20,
    )(*[pltpu.with_memory_space_constraint(x, pltpu.HBM) for x in (doc_lengths.reshape(1, -1), keys, values, q, g)])
    two = sent(kv, 2, 2)
    mixed = sent(kv, 1, 3)
    qg = lax.all_to_all(qg, "kvh", 0, 0, tiled=True)
    swapped = sent(two, 1, -1)
    units = len(UNITS)
    near, far = (two, mixed, kv), (swapped,)
    stat = shape((units, ROWS), jnp.float32)
    half = shape((units, len(near) * ROWS, ROWS), jnp.float32)
    p, d, top, total, inner = call(
        near_body, 2 + len(near), (half, half, stat, stat, stat), flops=1 << 30, vmem=4 << 20,
    )(first, qg, *near)
    p_two, p_mixed, p_swapped, own, dq = call(
        far_body,
        11,
        (shape(block),) * 3 + (shape(block, jnp.float32), shape((REPS, ROWS, 256))),
        scratch=(
            pltpu.VMEM((units, len(far) * ROWS, ROWS), jnp.float32),
            pltpu.VMEM((units, len(far) * ROWS, ROWS), jnp.float32),
            pltpu.VMEM((HEADS, 4 * ROWS, REPS * ROWS), jnp.bfloat16),
            pltpu.VMEM((HEADS, 4 * ROWS, REPS * ROWS), jnp.bfloat16),
        ),
        flops=1 << 30,
        vmem=16 << 20,
    )(first, top, total, inner, p, d, qg, *near, *far)
    from_swap = sent(p_swapped, 1, -1)
    from_mixed = sent(p_mixed, -3, -1)
    p_two = call(add_body, 2, shape(block), vmem=4 << 20)(p_two, from_swap)
    from_two = sent(p_two, -2, -2)
    dq = lax.all_to_all(dq, "kvh", 0, 0, tiled=True)
    dk, dv, dq = call(
        finish_body, 4, (shape((ROWS, 256)), shape((ROWS, 256)), shape((1, ROWS, 1024))), vmem=8 << 20,
    )(own, from_mixed, from_two, dq)
    return jnp.transpose(dq, (1, 0, 2)), dk, dv


def solution(mesh):
    in_specs = (P("ctx", "kvh", None), P("ctx", "kvh"), P("ctx", "kvh"), P("ctx", "kvh", None), P())
    out_specs = (P("ctx", "kvh", None), P("ctx", "kvh"), P("ctx", "kvh"))
    return jax.shard_map(
        per_device, mesh=mesh, in_specs=in_specs, out_specs=out_specs, check_vma=False
    )
```

time: 70.7 us -> 55.4 us (0.78)
  the two profiles are of different devices: /device:TPU:205 before, /device:TPU:110 now
where the time goes in v2:
time: 55.4 us; the launch traced here: 55 us
  starting transfers between devices  25.2 us (45%)
  waiting for transfers between devices  17.6 us (32%)
  Pallas kernels  11.5 us (21%)
  between operations  0.72 us (1%)
    ppermute x6, waiting for transfers between devices, sent(): lax.ppermute(value, 'ctx', [(i, j) for i, j in moves if 0 <= j < length])  16.7 us
    ppermute x6, starting transfers between devices, sent(): lax.ppermute(value, 'ctx', [(i, j) for i, j in moves if 0 <= j < length])  15.5 us
    pallas_call x1, Pallas kernels, per_device(): call(far_body, 11, (shape(block),) * 3 + (shape(block, jnp.float32), shap...  5.66 us
    all_to_all x1, starting transfers between devices, per_device(): qg = lax.all_to_all(qg, 'kvh', 0, 0, tiled=True)  4.92 us
    all_to_all x1, starting transfers between devices, per_device(): dq = lax.all_to_all(dq, 'kvh', 0, 0, tiled=True)  4.81 us
    pallas_call x1, Pallas kernels, per_device(): call(pack_body, 5, (shape(block), shape((REPS, 2, ROWS, 256)), shape((1,...  2.4 us
    pallas_call x1, Pallas kernels, per_device(): call(near_body, 2 + len(near), (half, half, stat, stat, stat), flops=1 <<...  2.36 us
  transfers between devices with their start and end apart: 8, of which 4 were waited for; matrix products, arithmetic and copies ran while one was open for 0% of the time, Pallas kernels for 4%

profile of v2, /device:TPU:110, one launch (start us, length us, event | category | flops | bytes accessed | tf_op | source)
XLA Modules:
  0.0 55.0 jit_solution(4335743728366129265)
XLA Ops:
  0.6 2.4 %shard_map.76 = (bf16[2,256,256]{2,1,0:T(8,128)(2,1)S(1)}, bf16[4,2,256,256]{3,2,1,0:T(8,128)(2,1)}, s32[1,256]{1,0:T(1,128)S(1)}) custom-call(s32[1,64]{1,0:T(1,128)} %bitcast.6, bf16[256,256]{1,0:T(8,128)(2,1)} %k_ref.1, bf16[256,256]{1,0:T(8,128)(2,1)} %v_ref.1, bf16[1,256,1024]{2,1,0:T(8,128)(2,1)} %bitcast.4, bf16[1,256,1024]{2,1,0:T(8,128)(2,1)} %bitcast.5), custom_call_target="tpu_custom_call" | custom-call | bytes 1048576 | tf_op jit(solution)/shard_map/pallas_call | solution.py:241
  3.0 4.9 %all-to-all-start = ((bf16[4,2,256,256]{3,2,1,0:T(8,128)(2,1)}), bf16[4,2,256,256]{3,2,1,0:T(8,128)(2,1)S(1)}, u32[]{:S(2)}, u32[]{:S(2)}) async-start(bf16[4,2,256,256]{3,2,1,0:T(8,128)(2,1)} %get-tuple-element.20), calls=%async_computation | async-start | bytes 2097152 | tf_op jit(solution)/shard_map/all_to_all | solution.py:258
  8.0 4.9 %collective-permute-start = (bf16[2,256,256]{2,1,0:T(8,128)(2,1)S(1)}, bf16[2,256,256]{2,1,0:T(8,128)(2,1)S(1)}, u32[]{:S(2)}, u32[]{:S(2)}) collective-permute-start(bf16[2,256,256]{2,1,0:T(8,128)(2,1)S(1)} %get-tuple-element.21.refs_2_), channel_id=1, source_target_pairs={{0,8},{4,12},{8,16},{12,20},{16,24},{20,28},{24,32},{28,36},{32,40... | collective-permute-start | bytes 786440 | tf_op jit(solution)/shard_map/ppermute | solution.py:32
  12.9 1.9 %collective-permute-start.1 = (bf16[2,256,256]{2,1,0:T(8,128)(2,1)S(1)}, bf16[2,256,256]{2,1,0:T(8,128)(2,1)S(1)}, u32[]{:S(2)}, u32[]{:S(2)}) collective-permute-start(bf16[2,256,256]{2,1,0:T(8,128)(2,1)S(1)} %get-tuple-element.21.refs_2_), channel_id=1, source_target_pairs={{0,4},{4,16},{8,12},{12,24},{16,20},{20,32},{24,28},{28,40},{32,36... | collective-permute-start | bytes 786440 | tf_op jit(solution)/shard_map/ppermute | solution.py:32
  14.8 5.3 %collective-permute-done.refs_0_ = bf16[2,256,256]{2,1,0:T(8,128)(2,1)S(1)} collective-permute-done((bf16[2,256,256]{2,1,0:T(8,128)(2,1)S(1)}, bf16[2,256,256]{2,1,0:T(8,128)(2,1)S(1)}, u32[]{:S(2)}, u32[]{:S(2)}) %collective-permute-start) | collective-permute-done | bytes 262176 | tf_op jit(solution)/shard_map/ppermute | solution.py:32
  20.1 1.9 %collective-permute-start.2 = (bf16[2,256,256]{2,1,0:T(8,128)(2,1)S(1)}, bf16[2,256,256]{2,1,0:T(8,128)(2,1)S(1)}, u32[]{:S(2)}, u32[]{:S(2)}) collective-permute-start(bf16[2,256,256]{2,1,0:T(8,128)(2,1)S(1)} %collective-permute-done.refs_0_), channel_id=1, source_target_pairs={{0,4},{4,0},{8,12},{12,8},{16,20},{20,16},{24,28},{28,24},{32,36},... | collective-permute-start | bytes 786440 | tf_op jit(solution)/shard_map/ppermute | solution.py:32
  22.1 0.0 collective-permute-done.1.refs_1_
  22.1 0.0 all-to-all-done.qg_ref
  22.1 2.4 %shard_map.77 = (f32[8,768,256]{2,1,0:T(8,128)S(1)}, f32[8,768,256]{2,1,0:T(8,128)S(1)}, f32[8,256]{1,0:T(8,128)S(1)}, f32[8,256]{1,0:T(8,128)S(1)}, f32[8,256]{1,0:T(8,128)S(1)}) custom-call(s32[1,256]{1,0:T(1,128)S(1)} %get-tuple-element.19.first_ref, bf16[4,2,256,256]{3,2,1,0:T(8,128)(2,1)S(1)} %all-to-all-done.qg_ref, ...), custom_call_target="tpu_custom_call" | custom-call | flops 1073741824 | bytes 1048576 | tf_op jit(solution)/shard_map/pallas_call | solution.py:264
  24.5 0.0 collective-permute-done.2.refs_3_
  24.5 5.7 %shard_map.78 = (bf16[2,256,256]{2,1,0:T(8,128)(2,1)S(1)}, bf16[2,256,256]{2,1,0:T(8,128)(2,1)S(1)}, bf16[2,256,256]{2,1,0:T(8,128)(2,1)S(1)}, f32[2,256,256]{2,1,0:T(8,128)S(1)}, bf16[4,256,256]{2,1,0:T(8,128)(2,1)}) custom-call(s32[1,256]{1,0:T(1,128)S(1)} %get-tuple-element.19.first_ref, f32[8,256]{1,0:T(8,128)S(1)} %get-tuple-element.22.top_ref, ...), custom_call_target="tpu_custom_call" | custom-call | flops 1073741824 | bytes 1048576 | tf_op jit(solution)/shard_map/pallas_call | solution.py:267
  30.1 2.4 %collective-permute-start.4 = (bf16[2,256,256]{2,1,0:T(8,128)(2,1)S(1)}, bf16[2,256,256]{2,1,0:T(8,128)(2,1)S(1)}, u32[]{:S(2)}, u32[]{:S(2)}) collective-permute-start(bf16[2,256,256]{2,1,0:T(8,128)(2,1)S(1)} %get-tuple-element.30), channel_id=1, source_target_pairs={{0,4},{4,0},{8,12},{12,8},{16,20},{20,16},{24,28},{28,24},{32,36},... | collective-permute-start | bytes 786440 | tf_op jit(solution)/shard_map/ppermute | solution.py:32
  32.5 4.8 %all-to-all-start.1 = ((bf16[4,256,256]{2,1,0:T(8,128)(2,1)}), bf16[4,256,256]{2,1,0:T(8,128)(2,1)S(1)}, u32[]{:S(2)}, u32[]{:S(2)}) async-start(bf16[4,256,256]{2,1,0:T(8,128)(2,1)} %get-tuple-element.31), calls=%async_computation.1 | async-start | bytes 1048576 | tf_op jit(solution)/shard_map/all_to_all | solution.py:284
  37.3 2.3 %collective-permute-start.3 = (bf16[2,256,256]{2,1,0:T(8,128)(2,1)S(1)}, bf16[2,256,256]{2,1,0:T(8,128)(2,1)S(1)}, u32[]{:S(2)}, u32[]{:S(2)}) collective-permute-start(bf16[2,256,256]{2,1,0:T(8,128)(2,1)S(1)} %get-tuple-element.28), channel_id=1, source_target_pairs={{4,0},{12,8},{16,4},{20,16},{24,12},{28,24},{32,20},{36,32},{40,28... | collective-permute-start | bytes 786440 | tf_op jit(solution)/shard_map/ppermute | solution.py:32
  39.6 0.0 collective-permute-done.4.b_ref
  39.6 0.1 shard_map.79
  39.7 2.1 %collective-permute-start.5 = (bf16[2,256,256]{2,1,0:T(8,128)(2,1)S(1)}, bf16[2,256,256]{2,1,0:T(8,128)(2,1)S(1)}, u32[]{:S(2)}, u32[]{:S(2)}) collective-permute-start(bf16[2,256,256]{2,1,0:T(8,128)(2,1)S(1)} %shard_map.79), channel_id=1, source_target_pairs={{8,0},{12,4},{16,8},{20,12},{24,16},{28,20},{32,24},{36,28},{40,32... | collective-permute-start | bytes 786440 | tf_op jit(solution)/shard_map/ppermute | solution.py:32
  41.8 2.9 %collective-permute-done.3.n1 = bf16[2,256,256]{2,1,0:T(8,128)(2,1)S(1)} collective-permute-done((bf16[2,256,256]{2,1,0:T(8,128)(2,1)S(1)}, bf16[2,256,256]{2,1,0:T(8,128)(2,1)S(1)}, u32[]{:S(2)}, u32[]{:S(2)}) %collective-permute-start.3) | collective-permute-done | bytes 262176 | tf_op jit(solution)/shard_map/ppermute | solution.py:32
  44.7 0.8 %all-to-all-done.1.dq_ref = bf16[4,256,256]{2,1,0:T(8,128)(2,1)S(1)} async-done(((bf16[4,256,256]{2,1,0:T(8,128)(2,1)}), bf16[4,256,256]{2,1,0:T(8,128)(2,1)S(1)}, u32[]{:S(2)}, u32[]{:S(2)}) %all-to-all-start.1) | async-done | bytes 524320 | tf_op jit(solution)/shard_map/all_to_all | solution.py:284
  45.5 8.4 %collective-permute-done.5.n2 = bf16[2,256,256]{2,1,0:T(8,128)(2,1)S(1)} collective-permute-done((bf16[2,256,256]{2,1,0:T(8,128)(2,1)S(1)}, bf16[2,256,256]{2,1,0:T(8,128)(2,1)S(1)}, u32[]{:S(2)}, u32[]{:S(2)}) %collective-permute-start.5) | collective-permute-done | bytes 262176 | tf_op jit(solution)/shard_map/ppermute | solution.py:32
  54.0 1.0 %shard_map.80 = (bf16[256,256]{1,0:T(8,128)(2,1)}, bf16[256,256]{1,0:T(8,128)(2,1)}, bf16[1,256,1024]{2,1,0:T(8,128)(2,1)}) custom-call(f32[2,256,256]{2,1,0:T(8,128)S(1)} %get-tuple-element.27.own, bf16[2,256,256]{2,1,0:T(8,128)(2,1)S(1)} %collective-permute-done.3.n1, bf16[2,256,256]{2,1,0:T(8,128)(2,1)S(1)} %collective-permute-done.5.n2, ...), custom_call_target="tpu_custom_call" | custom-call | bytes 1048576 | tf_op jit(solution)/shard_map/pallas_call | solution.py:285
Async XLA Ops:
  3.0 19.1 %all-to-all-start = ((bf16[4,2,256,256]{3,2,1,0:T(8,128)(2,1)}), bf16[4,2,256,256]{3,2,1,0:T(8,128)(2,1)S(1)}, u32[]{:S(2)}, u32[]{:S(2)}) async-start(bf16[4,2,256,256]{3,2,1,0:T(8,128)(2,1)} %get-tuple-element.20), calls=%async_computation | async-start | bytes 2097152 | tf_op jit(solution)/shard_map/all_to_all | solution.py:258
  8.0 12.2 %collective-permute-start = (bf16[2,256,256]{2,1,0:T(8,128)(2,1)S(1)}, bf16[2,256,256]{2,1,0:T(8,128)(2,1)S(1)}, u32[]{:S(2)}, u32[]{:S(2)}) collective-permute-start(bf16[2,256,256]{2,1,0:T(8,128)(2,1)S(1)} %get-tuple-element.21.refs_2_), channel_id=1, source_target_pairs={{0,8},{4,12},{8,16},{12,20},{16,24},{20,28},{24,32},{28,36},{32,40... | collective-permute-start | bytes 786440 | tf_op jit(solution)/shard_map/ppermute | solution.py:32
  12.9 9.2 %collective-permute-start.1 = (bf16[2,256,256]{2,1,0:T(8,128)(2,1)S(1)}, bf16[2,256,256]{2,1,0:T(8,128)(2,1)S(1)}, u32[]{:S(2)}, u32[]{:S(2)}) collective-permute-start(bf16[2,256,256]{2,1,0:T(8,128)(2,1)S(1)} %get-tuple-element.21.refs_2_), channel_id=1, source_target_pairs={{0,4},{4,16},{8,12},{12,24},{16,20},{20,32},{24,28},{28,40},{32,36... | collective-permute-start | bytes 786440 | tf_op jit(solution)/shard_map/ppermute | solution.py:32
  20.1 4.3 %collective-permute-start.2 = (bf16[2,256,256]{2,1,0:T(8,128)(2,1)S(1)}, bf16[2,256,256]{2,1,0:T(8,128)(2,1)S(1)}, u32[]{:S(2)}, u32[]{:S(2)}) collective-permute-start(bf16[2,256,256]{2,1,0:T(8,128)(2,1)S(1)} %collective-permute-done.refs_0_), channel_id=1, source_target_pairs={{0,4},{4,0},{8,12},{12,8},{16,20},{20,16},{24,28},{28,24},{32,36},... | collective-permute-start | bytes 786440 | tf_op jit(solution)/shard_map/ppermute | solution.py:32
  30.1 9.5 %collective-permute-start.4 = (bf16[2,256,256]{2,1,0:T(8,128)(2,1)S(1)}, bf16[2,256,256]{2,1,0:T(8,128)(2,1)S(1)}, u32[]{:S(2)}, u32[]{:S(2)}) collective-permute-start(bf16[2,256,256]{2,1,0:T(8,128)(2,1)S(1)} %get-tuple-element.30), channel_id=1, source_target_pairs={{0,4},{4,0},{8,12},{12,8},{16,20},{20,16},{24,28},{28,24},{32,36},... | collective-permute-start | bytes 786440 | tf_op jit(solution)/shard_map/ppermute | solution.py:32
  32.5 13.0 %all-to-all-start.1 = ((bf16[4,256,256]{2,1,0:T(8,128)(2,1)}), bf16[4,256,256]{2,1,0:T(8,128)(2,1)S(1)}, u32[]{:S(2)}, u32[]{:S(2)}) async-start(bf16[4,256,256]{2,1,0:T(8,128)(2,1)} %get-tuple-element.31), calls=%async_computation.1 | async-start | bytes 1048576 | tf_op jit(solution)/shard_map/all_to_all | solution.py:284
  37.3 7.4 %collective-permute-start.3 = (bf16[2,256,256]{2,1,0:T(8,128)(2,1)S(1)}, bf16[2,256,256]{2,1,0:T(8,128)(2,1)S(1)}, u32[]{:S(2)}, u32[]{:S(2)}) collective-permute-start(bf16[2,256,256]{2,1,0:T(8,128)(2,1)S(1)} %get-tuple-element.28), channel_id=1, source_target_pairs={{4,0},{12,8},{16,4},{20,16},{24,12},{28,24},{32,20},{36,32},{40,28... | collective-permute-start | bytes 786440 | tf_op jit(solution)/shard_map/ppermute | solution.py:32
  39.7 14.3 %collective-permute-start.5 = (bf16[2,256,256]{2,1,0:T(8,128)(2,1)S(1)}, bf16[2,256,256]{2,1,0:T(8,128)(2,1)S(1)}, u32[]{:S(2)}, u32[]{:S(2)}) collective-permute-start(bf16[2,256,256]{2,1,0:T(8,128)(2,1)S(1)} %shard_map.79), channel_id=1, source_target_pairs={{8,0},{12,4},{16,8},{20,12},{24,16},{28,20},{32,24},{36,28},{40,32... | collective-permute-start | bytes 786440 | tf_op jit(solution)/shard_map/ppermute | solution.py:32

commit v3 on v2

--- a/solution.py
+++ b/solution.py
@@ -40,24 +40,20 @@
     return pl.ds(b * ROWS, ROWS)
 
 
-def pack_body(len_ref, k_ref, v_ref, q_ref, g_ref, kv_ref, qg_ref, first_ref, len_buf, kv_buf, qg_buf, len_sem, sems):
+def pack_body(len_ref, k_ref, v_ref, q_ref, g_ref, kv_ref, qg_ref, first_ref, len_buf, len_sem, sems):
     moves = [
-        (ref.at[0, :, pl.ds(y * 256, 256)], qg_buf.at[y, a], qg_ref.at[y, a])
+        (ref.at[0, :, pl.ds(y * 256, 256)], qg_ref.at[y, a])
         for y in range(REPS)
         for a, ref in enumerate((q_ref, g_ref))
-    ] + [(ref, kv_buf.at[a], kv_ref.at[a]) for a, ref in enumerate((k_ref, v_ref))]
-    ins = [pltpu.make_async_copy(a, b, sems.at[0, n]) for n, (a, b, _) in enumerate(moves)]
-    outs = [pltpu.make_async_copy(b, c, sems.at[1, n]) for n, (_, b, c) in enumerate(moves)]
+    ] + [(ref, kv_ref.at[a]) for a, ref in enumerate((k_ref, v_ref))]
     lens = pltpu.make_async_copy(len_ref, len_buf, len_sem)
     lens.start()
-    for copy in ins:
+    copies = [pltpu.make_async_copy(a, b, sems.at[n]) for n, (a, b) in enumerate(moves)]
+    for copy in copies:
         copy.start()
     lens.wait()
     first_ref[...] = doc_first(len_buf, lax.axis_index("ctx") * ROWS)
-    for copy, after in zip(ins, outs):
-        copy.wait()
-        after.start()
-    for copy in outs:
+    for copy in copies:
         copy.wait()
 
 
@@ -203,15 +199,19 @@
 
 
 def add_body(a_ref, b_ref, c_ref):
-    c_ref[...] = (a_ref[...].astype(jnp.float32) + b_ref[...].astype(jnp.float32)).astype(jnp.bfloat16)
-
-
-def finish_body(own, n1, n2, dq_ref, k_ref, v_ref, q_ref):
-    total = own[...] + (n1[...].astype(jnp.float32) + n2[...].astype(jnp.float32))
-    k_ref[...] = total[0].astype(jnp.bfloat16)
-    v_ref[...] = total[1].astype(jnp.bfloat16)
+    other = b_ref[1 - lax.rem(lax.axis_index("ctx"), 2)]
+    c_ref[...] = (a_ref[...].astype(jnp.float32) + other.astype(jnp.float32)).astype(jnp.bfloat16)
+
+
+def rest_body(own, n1, dq_ref, sum_ref, q_ref):
+    sum_ref[...] = own[...] + n1[...].astype(jnp.float32)
     for y in range(REPS):
         q_ref[0, :, pl.ds(y * 256, 256)] = dq_ref[y]
+
+
+def finish_body(sum_ref, n2, k_ref, v_ref):
+    k_ref[...] = (sum_ref[0] + n2[0].astype(jnp.float32)).astype(jnp.bfloat16)
+    v_ref[...] = (sum_ref[1] + n2[1].astype(jnp.float32)).astype(jnp.bfloat16)
 
 
 VM = pl.BlockSpec(memory_space=pltpu.VMEM)
@@ -241,16 +241,14 @@
     kv, qg, first = call(
         pack_body,
         5,
-        (shape(block), shape((REPS, 2, ROWS, 256)), shape((1, ROWS), jnp.int32)),
+        (shape(block), pltpu.VMEM((REPS, 2, ROWS, 256), jnp.bfloat16), shape((1, ROWS), jnp.int32)),
         scratch=[
             pltpu.VMEM((1, doc_lengths.shape[0]), jnp.int32),
-            pltpu.VMEM(block, jnp.bfloat16),
-            pltpu.VMEM((REPS, 2, ROWS, 256), jnp.bfloat16),
             pltpu.SemaphoreType.DMA,
-            pltpu.SemaphoreType.DMA((2, 10)),
+            pltpu.SemaphoreType.DMA((10,)),
         ],
         spec=ANY,
-        ospec=(ANY, ANY, VM),
+        ospec=(VM, VM, VM),
         vmem=4 << 20,
     )(*[pltpu.with_memory_space_constraint(x, pltpu.HBM) for x in (doc_lengths.reshape(1, -1), keys, values, q, g)])
     two = sent(kv, 2, 2)
@@ -267,7 +265,7 @@
     p_two, p_mixed, p_swapped, own, dq = call(
         far_body,
         11,
-        (shape(block),) * 3 + (shape(block, jnp.float32), shape((REPS, ROWS, 256))),
+        (shape(block),) * 3 + (shape(block, jnp.float32), pltpu.VMEM((REPS, ROWS, 256), jnp.bfloat16)),
         scratch=(
             pltpu.VMEM((units, len(far) * ROWS, ROWS), jnp.float32),
             pltpu.VMEM((units, len(far) * ROWS, ROWS), jnp.float32),
@@ -277,14 +275,16 @@
         flops=1 << 30,
         vmem=16 << 20,
     )(first, top, total, inner, p, d, qg, *near, *far)
-    from_swap = sent(p_swapped, 1, -1)
+    pairs = [[i, i + 1] for i in range(0, lax.axis_size("ctx"), 2)]
+    from_swap = lax.all_gather(p_swapped, "ctx", axis_index_groups=pairs)
     from_mixed = sent(p_mixed, -3, -1)
     p_two = call(add_body, 2, shape(block), vmem=4 << 20)(p_two, from_swap)
     from_two = sent(p_two, -2, -2)
     dq = lax.all_to_all(dq, "kvh", 0, 0, tiled=True)
-    dk, dv, dq = call(
-        finish_body, 4, (shape((ROWS, 256)), shape((ROWS, 256)), shape((1, ROWS, 1024))), vmem=8 << 20,
-    )(own, from_mixed, from_two, dq)
+    own, dq = call(
+        rest_body, 3, (shape(block, jnp.float32), shape((1, ROWS, 1024))), vmem=4 << 20,
+    )(own, from_mixed, dq)
+    dk, dv = call(finish_body, 2, (shape((ROWS, 256)), shape((ROWS, 256))), vmem=4 << 20)(own, from_two)
     return jnp.transpose(dq, (1, 0, 2)), dk, dv
 
 

time: 55.4 us -> 54.2 us (0.978)
  blocking collectives: 0 us -> 2.31 us
  waiting for transfers between devices: 17.6 us -> 15.5 us
  starting transfers between devices: 25.2 us -> 23.2 us
  Pallas kernels: 11.5 us -> 12.2 us
    ppermute x6 -> x5, waiting for transfers between devices: 16.7 us -> 13.9 us  [sent(): lax.ppermute(value, 'ctx', [(i, j) for i, j in moves if 0 <= j < length])]
    all_gather x0 -> x1, blocking collectives: none -> 2.31 us  [per_device(): from_swap = lax.all_gather(p_swapped, 'ctx', axis_index_groups=pairs)]
    ppermute x6 -> x5, starting transfers between devices: 15.5 us -> 13.4 us  [sent(): lax.ppermute(value, 'ctx', [(i, j) for i, j in moves if 0 <= j < length])]
    all_to_all x1, waiting for transfers between devices: 0.82 us -> 1.58 us  [per_device(): dq = lax.all_to_all(dq, 'kvh', 0, 0, tiled=True)]
    pallas_call x3 -> x4, Pallas kernels: 9.05 us -> 9.74 us  [the longest x1 5.66 us: per_device(): call(far_body, 11, (shape(block),) * 3 + (shape(block, jnp.float32), pltp...]
  transfers between devices with their start and end apart: 8 -> 7, of which waited for: 4 -> 3; matrix products, arithmetic and copies ran while one was open for 0% -> 0% of each run, Pallas kernels for 4% -> 6%
where the time goes in v3:
time: 54.2 us; the launch traced here: 53.8 us
  starting transfers between devices  23.2 us (43%)
  waiting for transfers between devices  15.5 us (29%)
  Pallas kernels  12.2 us (23%)
  blocking collectives  2.31 us (4%)
  between operations  0.71 us (1%)
    ppermute x5, waiting for transfers between devices, sent(): lax.ppermute(value, 'ctx', [(i, j) for i, j in moves if 0 <= j < length])  13.9 us
    ppermute x5, starting transfers between devices, sent(): lax.ppermute(value, 'ctx', [(i, j) for i, j in moves if 0 <= j < length])  13.4 us
    pallas_call x1, Pallas kernels, per_device(): call(far_body, 11, (shape(block),) * 3 + (shape(block, jnp.float32), pltp...  5.66 us
    all_to_all x1, starting transfers between devices, per_device(): qg = lax.all_to_all(qg, 'kvh', 0, 0, tiled=True)  4.92 us
    all_to_all x1, starting transfers between devices, per_device(): dq = lax.all_to_all(dq, 'kvh', 0, 0, tiled=True)  4.81 us
    pallas_call x1, Pallas kernels, per_device(): call(pack_body, 5, (shape(block), pltpu.VMEM((REPS, 2, ROWS, 256), jnp.bf...  2.45 us
    pallas_call x1, Pallas kernels, per_device(): call(near_body, 2 + len(near), (half, half, stat, stat, stat), flops=1 <<...  2.35 us
    all_gather x1, blocking collectives, per_device(): from_swap = lax.all_gather(p_swapped, 'ctx', axis_index_groups=pairs)  2.31 us
  transfers between devices with their start and end apart: 7, of which 3 were waited for; matrix products, arithmetic and copies ran while one was open for 0% of the time, Pallas kernels for 6%

profile of v3, /device:TPU:110, one launch (start us, length us, event | category | flops | bytes accessed | tf_op | source)
XLA Modules:
  0.0 53.8 jit_solution(6161599360906576216)
XLA Ops:
  0.6 2.4 %shard_map.76 = (bf16[2,256,256]{2,1,0:T(8,128)(2,1)S(1)}, bf16[4,2,256,256]{3,2,1,0:T(8,128)(2,1)}, s32[1,256]{1,0:T(1,128)S(1)}) custom-call(s32[1,64]{1,0:T(1,128)} %bitcast.8, bf16[256,256]{1,0:T(8,128)(2,1)} %k_ref.1, bf16[256,256]{1,0:T(8,128)(2,1)} %v_ref.1, bf16[1,256,1024]{2,1,0:T(8,128)(2,1)} %bitcast.6, bf16[1,256,1024]{2,1,0:T(8,128)(2,1)} %bitcast.7), custom_call_target="tpu_custom_call" | custom-call | bytes 1048576 | tf_op jit(solution)/shard_map/pallas_call | solution.py:241
  3.1 4.9 %all-to-all-start = ((bf16[4,2,256,256]{3,2,1,0:T(8,128)(2,1)}), bf16[4,2,256,256]{3,2,1,0:T(8,128)(2,1)S(1)}, u32[]{:S(2)}, u32[]{:S(2)}) async-start(bf16[4,2,256,256]{3,2,1,0:T(8,128)(2,1)} %get-tuple-element.21), calls=%async_computation | async-start | bytes 2097152 | tf_op jit(solution)/shard_map/all_to_all | solution.py:256
  8.0 4.9 %collective-permute-start = (bf16[2,256,256]{2,1,0:T(8,128)(2,1)S(1)}, bf16[2,256,256]{2,1,0:T(8,128)(2,1)S(1)}, u32[]{:S(2)}, u32[]{:S(2)}) collective-permute-start(bf16[2,256,256]{2,1,0:T(8,128)(2,1)S(1)} %get-tuple-element.22.refs_2_), channel_id=1, source_target_pairs={{0,8},{4,12},{8,16},{12,20},{16,24},{20,28},{24,32},{28,36},{32,40... | collective-permute-start | bytes 786440 | tf_op jit(solution)/shard_map/ppermute | solution.py:32
  13.0 1.9 %collective-permute-start.1 = (bf16[2,256,256]{2,1,0:T(8,128)(2,1)S(1)}, bf16[2,256,256]{2,1,0:T(8,128)(2,1)S(1)}, u32[]{:S(2)}, u32[]{:S(2)}) collective-permute-start(bf16[2,256,256]{2,1,0:T(8,128)(2,1)S(1)} %get-tuple-element.22.refs_2_), channel_id=1, source_target_pairs={{0,4},{4,16},{8,12},{12,24},{16,20},{20,32},{24,28},{28,40},{32,36... | collective-permute-start | bytes 786440 | tf_op jit(solution)/shard_map/ppermute | solution.py:32
  14.9 5.3 %collective-permute-done.refs_0_ = bf16[2,256,256]{2,1,0:T(8,128)(2,1)S(1)} collective-permute-done((bf16[2,256,256]{2,1,0:T(8,128)(2,1)S(1)}, bf16[2,256,256]{2,1,0:T(8,128)(2,1)S(1)}, u32[]{:S(2)}, u32[]{:S(2)}) %collective-permute-start) | collective-permute-done | bytes 262176 | tf_op jit(solution)/shard_map/ppermute | solution.py:32
  20.2 1.9 %collective-permute-start.2 = (bf16[2,256,256]{2,1,0:T(8,128)(2,1)S(1)}, bf16[2,256,256]{2,1,0:T(8,128)(2,1)S(1)}, u32[]{:S(2)}, u32[]{:S(2)}) collective-permute-start(bf16[2,256,256]{2,1,0:T(8,128)(2,1)S(1)} %collective-permute-done.refs_0_), channel_id=1, source_target_pairs={{0,4},{4,0},{8,12},{12,8},{16,20},{20,16},{24,28},{28,24},{32,36},... | collective-permute-start | bytes 786440 | tf_op jit(solution)/shard_map/ppermute | solution.py:32
  22.1 0.0 collective-permute-done.1.refs_1_
  22.2 0.0 all-to-all-done.qg_ref
  22.2 2.4 %shard_map.77 = (f32[8,768,256]{2,1,0:T(8,128)S(1)}, f32[8,768,256]{2,1,0:T(8,128)S(1)}, f32[8,256]{1,0:T(8,128)S(1)}, f32[8,256]{1,0:T(8,128)S(1)}, f32[8,256]{1,0:T(8,128)S(1)}) custom-call(s32[1,256]{1,0:T(1,128)S(1)} %get-tuple-element.20.first_ref, bf16[4,2,256,256]{3,2,1,0:T(8,128)(2,1)S(1)} %all-to-all-done.qg_ref, ...), custom_call_target="tpu_custom_call" | custom-call | flops 1073741824 | bytes 1048576 | tf_op jit(solution)/shard_map/pallas_call | solution.py:262
  24.5 0.0 collective-permute-done.2.refs_3_
  24.5 5.7 %shard_map.78 = (bf16[2,256,256]{2,1,0:T(8,128)(2,1)S(1)}, bf16[2,256,256]{2,1,0:T(8,128)(2,1)S(1)}, bf16[2,256,256]{2,1,0:T(8,128)(2,1)S(1)}, f32[2,256,256]{2,1,0:T(8,128)S(1)}, bf16[4,256,256]{2,1,0:T(8,128)(2,1)}) custom-call(s32[1,256]{1,0:T(1,128)S(1)} %get-tuple-element.20.first_ref, f32[8,256]{1,0:T(8,128)S(1)} %get-tuple-element.23.top_ref, ...), custom_call_target="tpu_custom_call" | custom-call | flops 1073741824 | bytes 1048576 | tf_op jit(solution)/shard_map/pallas_call | solution.py:265
  30.2 4.8 %all-to-all-start.1 = ((bf16[4,256,256]{2,1,0:T(8,128)(2,1)}), bf16[4,256,256]{2,1,0:T(8,128)(2,1)S(1)}, u32[]{:S(2)}, u32[]{:S(2)}) async-start(bf16[4,256,256]{2,1,0:T(8,128)(2,1)} %get-tuple-element.30), calls=%async_computation.1 | async-start | bytes 1048576 | tf_op jit(solution)/shard_map/all_to_all | solution.py:283
  35.0 1.9 %collective-permute-start.3 = (bf16[2,256,256]{2,1,0:T(8,128)(2,1)S(1)}, bf16[2,256,256]{2,1,0:T(8,128)(2,1)S(1)}, u32[]{:S(2)}, u32[]{:S(2)}) collective-permute-start(bf16[2,256,256]{2,1,0:T(8,128)(2,1)S(1)} %get-tuple-element.29), channel_id=1, source_target_pairs={{4,0},{12,8},{16,4},{20,16},{24,12},{28,24},{32,20},{36,32},{40,28... | collective-permute-start | bytes 786440 | tf_op jit(solution)/shard_map/ppermute | solution.py:32
  36.9 2.3 %all-gather = bf16[4,256,256]{2,1,0:T(8,128)(2,1)S(1)} all-gather(bf16[2,256,256]{2,1,0:T(8,128)(2,1)S(1)} %get-tuple-element.34), channel_id=2, replica_groups={{0,4},{8,12},{16,20},{24,28},{32,36},{40,44},{48,52},{56,60},{64,68},{7..., dimensions={0}, use_global_device_ids=true | all-gather | bytes 786432 | tf_op jit(solution)/shard_map/all_gather | solution.py:279
  39.2 0.1 shard_map.80
  39.3 2.7 %collective-permute-start.4 = (bf16[2,256,256]{2,1,0:T(8,128)(2,1)S(1)}, bf16[2,256,256]{2,1,0:T(8,128)(2,1)S(1)}, u32[]{:S(2)}, u32[]{:S(2)}) collective-permute-start(bf16[2,256,256]{2,1,0:T(8,128)(2,1)S(1)} %shard_map.80), channel_id=1, source_target_pairs={{8,0},{12,4},{16,8},{20,12},{24,16},{28,20},{32,24},{36,28},{40,32... | collective-permute-start | bytes 786440 | tf_op jit(solution)/shard_map/ppermute | solution.py:32
  42.1 0.0 collective-permute-done.3.n1
  42.1 1.6 %all-to-all-done.1.dq_ref = bf16[4,256,256]{2,1,0:T(8,128)(2,1)S(1)} async-done(((bf16[4,256,256]{2,1,0:T(8,128)(2,1)}), bf16[4,256,256]{2,1,0:T(8,128)(2,1)S(1)}, u32[]{:S(2)}, u32[]{:S(2)}) %all-to-all-start.1) | async-done | bytes 524320 | tf_op jit(solution)/shard_map/all_to_all | solution.py:283
  43.6 0.9 %shard_map.79 = (f32[2,256,256]{2,1,0:T(8,128)S(1)}, bf16[1,256,1024]{2,1,0:T(8,128)(2,1)}) custom-call(f32[2,256,256]{2,1,0:T(8,128)S(1)} %get-tuple-element.28.own, bf16[2,256,256]{2,1,0:T(8,128)(2,1)S(1)} %collective-permute-done.3.n1, bf16[4,256,256]{2,1,0:T(8,128)(2,1)S(1)} %all-to-all-done.1.dq_ref), custom_call_target="tpu_custom_call" | custom-call | bytes 1048576 | tf_op jit(solution)/shard_map/pallas_call | solution.py:284
  44.5 8.6 %collective-permute-done.4.n2 = bf16[2,256,256]{2,1,0:T(8,128)(2,1)S(1)} collective-permute-done((bf16[2,256,256]{2,1,0:T(8,128)(2,1)S(1)}, bf16[2,256,256]{2,1,0:T(8,128)(2,1)S(1)}, u32[]{:S(2)}, u32[]{:S(2)}) %collective-permute-start.4) | collective-permute-done | bytes 262176 | tf_op jit(solution)/shard_map/ppermute | solution.py:32
  53.1 0.7 %shard_map.81 = (bf16[256,256]{1,0:T(8,128)(2,1)}, bf16[256,256]{1,0:T(8,128)(2,1)}) custom-call(f32[2,256,256]{2,1,0:T(8,128)S(1)} %get-tuple-element.32.sum_ref, bf16[2,256,256]{2,1,0:T(8,128)(2,1)S(1)} %collective-permute-done.4.n2), custom_call_target="tpu_custom_call" | custom-call | bytes 1048576 | tf_op jit(solution)/shard_map/pallas_call | solution.py:287
Async XLA Ops:
  3.1 19.1 %all-to-all-start = ((bf16[4,2,256,256]{3,2,1,0:T(8,128)(2,1)}), bf16[4,2,256,256]{3,2,1,0:T(8,128)(2,1)S(1)}, u32[]{:S(2)}, u32[]{:S(2)}) async-start(bf16[4,2,256,256]{3,2,1,0:T(8,128)(2,1)} %get-tuple-element.21), calls=%async_computation | async-start | bytes 2097152 | tf_op jit(solution)/shard_map/all_to_all | solution.py:256
  8.0 12.2 %collective-permute-start = (bf16[2,256,256]{2,1,0:T(8,128)(2,1)S(1)}, bf16[2,256,256]{2,1,0:T(8,128)(2,1)S(1)}, u32[]{:S(2)}, u32[]{:S(2)}) collective-permute-start(bf16[2,256,256]{2,1,0:T(8,128)(2,1)S(1)} %get-tuple-element.22.refs_2_), channel_id=1, source_target_pairs={{0,8},{4,12},{8,16},{12,20},{16,24},{20,28},{24,32},{28,36},{32,40... | collective-permute-start | bytes 786440 | tf_op jit(solution)/shard_map/ppermute | solution.py:32
  13.0 9.2 %collective-permute-start.1 = (bf16[2,256,256]{2,1,0:T(8,128)(2,1)S(1)}, bf16[2,256,256]{2,1,0:T(8,128)(2,1)S(1)}, u32[]{:S(2)}, u32[]{:S(2)}) collective-permute-start(bf16[2,256,256]{2,1,0:T(8,128)(2,1)S(1)} %get-tuple-element.22.refs_2_), channel_id=1, source_target_pairs={{0,4},{4,16},{8,12},{12,24},{16,20},{20,32},{24,28},{28,40},{32,36... | collective-permute-start | bytes 786440 | tf_op jit(solution)/shard_map/ppermute | solution.py:32
  20.2 4.3 %collective-permute-start.2 = (bf16[2,256,256]{2,1,0:T(8,128)(2,1)S(1)}, bf16[2,256,256]{2,1,0:T(8,128)(2,1)S(1)}, u32[]{:S(2)}, u32[]{:S(2)}) collective-permute-start(bf16[2,256,256]{2,1,0:T(8,128)(2,1)S(1)} %collective-permute-done.refs_0_), channel_id=1, source_target_pairs={{0,4},{4,0},{8,12},{12,8},{16,20},{20,16},{24,28},{28,24},{32,36},... | collective-permute-start | bytes 786440 | tf_op jit(solution)/shard_map/ppermute | solution.py:32
  30.2 13.5 %all-to-all-start.1 = ((bf16[4,256,256]{2,1,0:T(8,128)(2,1)}), bf16[4,256,256]{2,1,0:T(8,128)(2,1)S(1)}, u32[]{:S(2)}, u32[]{:S(2)}) async-start(bf16[4,256,256]{2,1,0:T(8,128)(2,1)} %get-tuple-element.30), calls=%async_computation.1 | async-start | bytes 1048576 | tf_op jit(solution)/shard_map/all_to_all | solution.py:283
  35.0 7.1 %collective-permute-start.3 = (bf16[2,256,256]{2,1,0:T(8,128)(2,1)S(1)}, bf16[2,256,256]{2,1,0:T(8,128)(2,1)S(1)}, u32[]{:S(2)}, u32[]{:S(2)}) collective-permute-start(bf16[2,256,256]{2,1,0:T(8,128)(2,1)S(1)} %get-tuple-element.29), channel_id=1, source_target_pairs={{4,0},{12,8},{16,4},{20,16},{24,12},{28,24},{32,20},{36,32},{40,28... | collective-permute-start | bytes 786440 | tf_op jit(solution)/shard_map/ppermute | solution.py:32
  39.3 13.8 %collective-permute-start.4 = (bf16[2,256,256]{2,1,0:T(8,128)(2,1)S(1)}, bf16[2,256,256]{2,1,0:T(8,128)(2,1)S(1)}, u32[]{:S(2)}, u32[]{:S(2)}) collective-permute-start(bf16[2,256,256]{2,1,0:T(8,128)(2,1)S(1)} %shard_map.80), channel_id=1, source_target_pairs={{8,0},{12,4},{16,8},{20,12},{24,16},{28,20},{32,24},{36,28},{40,32... | collective-permute-start | bytes 786440 | tf_op jit(solution)/shard_map/ppermute | solution.py:32

commit v4 on v3

--- a/solution.py
+++ b/solution.py
@@ -177,8 +177,21 @@
     def gather(h, b):
         queries = jnp.concatenate([qg_ref[r, 0, :, cols(h)] for r in range(REPS)], axis=0)
         grads = jnp.concatenate([qg_ref[r, 1, :, cols(h)] for r in range(REPS)], axis=0)
-        dk = dot(t_ref[h, block_rows(b), :], queries, NN) * SCALE
-        dv = dot(w_ref[h, block_rows(b), :], grads, NN)
+        if b == near - 1:
+            half = ROWS // 2
+            low_rows = pl.ds(b * ROWS, half)
+            late = [pl.ds(r * ROWS + half, half) for r in range(REPS)]
+            high = pl.ds(b * ROWS + half, half)
+
+            def both(ref, other, a):
+                cut = jnp.concatenate([ref[h, high, at] for at in late], axis=1)
+                rows = jnp.concatenate([qg_ref[r, a, pl.ds(half, half), cols(h)] for r in range(REPS)], axis=0)
+                return jnp.concatenate([dot(ref[h, low_rows, :], other, NN), dot(cut, rows, NN)], axis=0)
+
+            dk, dv = both(t_ref, queries, 0) * SCALE, both(w_ref, grads, 1)
+        else:
+            dk = dot(t_ref[h, block_rows(b), :], queries, NN) * SCALE
+            dv = dot(w_ref[h, block_rows(b), :], grads, NN)
         outs[b][0, :, cols(h)] = dk.astype(outs[b].dtype)
         outs[b][1, :, cols(h)] = dv.astype(outs[b].dtype)
 

time: 54.2 us -> 54.4 us (level)
  no operation moved by 1% of the time
where the time goes in v4:
time: 54.4 us; the launch traced here: 54 us
  starting transfers between devices  23.2 us (43%)
  waiting for transfers between devices  15.5 us (28%)
  Pallas kernels  12.3 us (23%)
  blocking collectives  2.31 us (4%)
  between operations  0.71 us (1%)
    ppermute x5, waiting for transfers between devices, sent(): lax.ppermute(value, 'ctx', [(i, j) for i, j in moves if 0 <= j < length])  13.9 us
    ppermute x5, starting transfers between devices, sent(): lax.ppermute(value, 'ctx', [(i, j) for i, j in moves if 0 <= j < length])  13.4 us
    pallas_call x1, Pallas kernels, per_device(): call(far_body, 11, (shape(block),) * 3 + (shape(block, jnp.float32), pltp...  5.83 us
    all_to_all x1, starting transfers between devices, per_device(): qg = lax.all_to_all(qg, 'kvh', 0, 0, tiled=True)  4.92 us
    all_to_all x1, starting transfers between devices, per_device(): dq = lax.all_to_all(dq, 'kvh', 0, 0, tiled=True)  4.8 us
    pallas_call x1, Pallas kernels, per_device(): call(pack_body, 5, (shape(block), pltpu.VMEM((REPS, 2, ROWS, 256), jnp.bf...  2.45 us
    pallas_call x1, Pallas kernels, per_device(): call(near_body, 2 + len(near), (half, half, stat, stat, stat), flops=1 <<...  2.35 us
    all_gather x1, blocking collectives, per_device(): from_swap = lax.all_gather(p_swapped, 'ctx', axis_index_groups=pairs)  2.31 us
  transfers between devices with their start and end apart: 7, of which 3 were waited for; matrix products, arithmetic and copies ran while one was open for 0% of the time, Pallas kernels for 6%

profile of v4, /device:TPU:110, one launch (start us, length us, event | category | flops | bytes accessed | tf_op | source)
XLA Modules:
  0.0 54.0 jit_solution(6198857990915617164)
XLA Ops:
  0.6 2.4 %shard_map.76 = (bf16[2,256,256]{2,1,0:T(8,128)(2,1)S(1)}, bf16[4,2,256,256]{3,2,1,0:T(8,128)(2,1)}, s32[1,256]{1,0:T(1,128)S(1)}) custom-call(s32[1,64]{1,0:T(1,128)} %bitcast.8, bf16[256,256]{1,0:T(8,128)(2,1)} %k_ref.1, bf16[256,256]{1,0:T(8,128)(2,1)} %v_ref.1, bf16[1,256,1024]{2,1,0:T(8,128)(2,1)} %bitcast.6, bf16[1,256,1024]{2,1,0:T(8,128)(2,1)} %bitcast.7), custom_call_target="tpu_custom_call" | custom-call | bytes 1048576 | tf_op jit(solution)/shard_map/pallas_call | solution.py:254
  3.1 4.9 %all-to-all-start = ((bf16[4,2,256,256]{3,2,1,0:T(8,128)(2,1)}), bf16[4,2,256,256]{3,2,1,0:T(8,128)(2,1)S(1)}, u32[]{:S(2)}, u32[]{:S(2)}) async-start(bf16[4,2,256,256]{3,2,1,0:T(8,128)(2,1)} %get-tuple-element.21), calls=%async_computation | async-start | bytes 2097152 | tf_op jit(solution)/shard_map/all_to_all | solution.py:269
  8.0 4.9 %collective-permute-start = (bf16[2,256,256]{2,1,0:T(8,128)(2,1)S(1)}, bf16[2,256,256]{2,1,0:T(8,128)(2,1)S(1)}, u32[]{:S(2)}, u32[]{:S(2)}) collective-permute-start(bf16[2,256,256]{2,1,0:T(8,128)(2,1)S(1)} %get-tuple-element.22.refs_2_), channel_id=1, source_target_pairs={{0,8},{4,12},{8,16},{12,20},{16,24},{20,28},{24,32},{28,36},{32,40... | collective-permute-start | bytes 786440 | tf_op jit(solution)/shard_map/ppermute | solution.py:32
  13.0 1.9 %collective-permute-start.1 = (bf16[2,256,256]{2,1,0:T(8,128)(2,1)S(1)}, bf16[2,256,256]{2,1,0:T(8,128)(2,1)S(1)}, u32[]{:S(2)}, u32[]{:S(2)}) collective-permute-start(bf16[2,256,256]{2,1,0:T(8,128)(2,1)S(1)} %get-tuple-element.22.refs_2_), channel_id=1, source_target_pairs={{0,4},{4,16},{8,12},{12,24},{16,20},{20,32},{24,28},{28,40},{32,36... | collective-permute-start | bytes 786440 | tf_op jit(solution)/shard_map/ppermute | solution.py:32
  14.9 5.3 %collective-permute-done.refs_0_ = bf16[2,256,256]{2,1,0:T(8,128)(2,1)S(1)} collective-permute-done((bf16[2,256,256]{2,1,0:T(8,128)(2,1)S(1)}, bf16[2,256,256]{2,1,0:T(8,128)(2,1)S(1)}, u32[]{:S(2)}, u32[]{:S(2)}) %collective-permute-start) | collective-permute-done | bytes 262176 | tf_op jit(solution)/shard_map/ppermute | solution.py:32
  20.2 1.9 %collective-permute-start.2 = (bf16[2,256,256]{2,1,0:T(8,128)(2,1)S(1)}, bf16[2,256,256]{2,1,0:T(8,128)(2,1)S(1)}, u32[]{:S(2)}, u32[]{:S(2)}) collective-permute-start(bf16[2,256,256]{2,1,0:T(8,128)(2,1)S(1)} %collective-permute-done.refs_0_), channel_id=1, source_target_pairs={{0,4},{4,0},{8,12},{12,8},{16,20},{20,16},{24,28},{28,24},{32,36},... | collective-permute-start | bytes 786440 | tf_op jit(solution)/shard_map/ppermute | solution.py:32
  22.1 0.0 collective-permute-done.1.refs_1_
  22.2 0.0 all-to-all-done.qg_ref
  22.2 2.4 %shard_map.77 = (f32[8,768,256]{2,1,0:T(8,128)S(1)}, f32[8,768,256]{2,1,0:T(8,128)S(1)}, f32[8,256]{1,0:T(8,128)S(1)}, f32[8,256]{1,0:T(8,128)S(1)}, f32[8,256]{1,0:T(8,128)S(1)}) custom-call(s32[1,256]{1,0:T(1,128)S(1)} %get-tuple-element.20.first_ref, bf16[4,2,256,256]{3,2,1,0:T(8,128)(2,1)S(1)} %all-to-all-done.qg_ref, ...), custom_call_target="tpu_custom_call" | custom-call | flops 1073741824 | bytes 1048576 | tf_op jit(solution)/shard_map/pallas_call | solution.py:275
  24.5 0.0 collective-permute-done.2.refs_3_
  24.5 5.8 %shard_map.78 = (bf16[2,256,256]{2,1,0:T(8,128)(2,1)S(1)}, bf16[2,256,256]{2,1,0:T(8,128)(2,1)S(1)}, bf16[2,256,256]{2,1,0:T(8,128)(2,1)S(1)}, f32[2,256,256]{2,1,0:T(8,128)S(1)}, bf16[4,256,256]{2,1,0:T(8,128)(2,1)}) custom-call(s32[1,256]{1,0:T(1,128)S(1)} %get-tuple-element.20.first_ref, f32[8,256]{1,0:T(8,128)S(1)} %get-tuple-element.23.top_ref, ...), custom_call_target="tpu_custom_call" | custom-call | flops 1073741824 | bytes 1048576 | tf_op jit(solution)/shard_map/pallas_call | solution.py:278
  30.4 4.8 %all-to-all-start.1 = ((bf16[4,256,256]{2,1,0:T(8,128)(2,1)}), bf16[4,256,256]{2,1,0:T(8,128)(2,1)S(1)}, u32[]{:S(2)}, u32[]{:S(2)}) async-start(bf16[4,256,256]{2,1,0:T(8,128)(2,1)} %get-tuple-element.30), calls=%async_computation.1 | async-start | bytes 1048576 | tf_op jit(solution)/shard_map/all_to_all | solution.py:296
  35.2 1.9 %collective-permute-start.3 = (bf16[2,256,256]{2,1,0:T(8,128)(2,1)S(1)}, bf16[2,256,256]{2,1,0:T(8,128)(2,1)S(1)}, u32[]{:S(2)}, u32[]{:S(2)}) collective-permute-start(bf16[2,256,256]{2,1,0:T(8,128)(2,1)S(1)} %get-tuple-element.29), channel_id=1, source_target_pairs={{4,0},{12,8},{16,4},{20,16},{24,12},{28,24},{32,20},{36,32},{40,28... | collective-permute-start | bytes 786440 | tf_op jit(solution)/shard_map/ppermute | solution.py:32
  37.1 2.3 %all-gather = bf16[4,256,256]{2,1,0:T(8,128)(2,1)S(1)} all-gather(bf16[2,256,256]{2,1,0:T(8,128)(2,1)S(1)} %get-tuple-element.34), channel_id=2, replica_groups={{0,4},{8,12},{16,20},{24,28},{32,36},{40,44},{48,52},{56,60},{64,68},{7..., dimensions={0}, use_global_device_ids=true | all-gather | bytes 786432 | tf_op jit(solution)/shard_map/all_gather | solution.py:292
  39.4 0.1 shard_map.80
  39.5 2.8 %collective-permute-start.4 = (bf16[2,256,256]{2,1,0:T(8,128)(2,1)S(1)}, bf16[2,256,256]{2,1,0:T(8,128)(2,1)S(1)}, u32[]{:S(2)}, u32[]{:S(2)}) collective-permute-start(bf16[2,256,256]{2,1,0:T(8,128)(2,1)S(1)} %shard_map.80), channel_id=1, source_target_pairs={{8,0},{12,4},{16,8},{20,12},{24,16},{28,20},{32,24},{36,28},{40,32... | collective-permute-start | bytes 786440 | tf_op jit(solution)/shard_map/ppermute | solution.py:32
  42.2 0.0 collective-permute-done.3.n1
  42.2 1.6 %all-to-all-done.1.dq_ref = bf16[4,256,256]{2,1,0:T(8,128)(2,1)S(1)} async-done(((bf16[4,256,256]{2,1,0:T(8,128)(2,1)}), bf16[4,256,256]{2,1,0:T(8,128)(2,1)S(1)}, u32[]{:S(2)}, u32[]{:S(2)}) %all-to-all-start.1) | async-done | bytes 524320 | tf_op jit(solution)/shard_map/all_to_all | solution.py:296
  43.8 0.9 %shard_map.79 = (f32[2,256,256]{2,1,0:T(8,128)S(1)}, bf16[1,256,1024]{2,1,0:T(8,128)(2,1)}) custom-call(f32[2,256,256]{2,1,0:T(8,128)S(1)} %get-tuple-element.28.own, bf16[2,256,256]{2,1,0:T(8,128)(2,1)S(1)} %collective-permute-done.3.n1, bf16[4,256,256]{2,1,0:T(8,128)(2,1)S(1)} %all-to-all-done.1.dq_ref), custom_call_target="tpu_custom_call" | custom-call | bytes 1048576 | tf_op jit(solution)/shard_map/pallas_call | solution.py:297
  44.7 8.5 %collective-permute-done.4.n2 = bf16[2,256,256]{2,1,0:T(8,128)(2,1)S(1)} collective-permute-done((bf16[2,256,256]{2,1,0:T(8,128)(2,1)S(1)}, bf16[2,256,256]{2,1,0:T(8,128)(2,1)S(1)}, u32[]{:S(2)}, u32[]{:S(2)}) %collective-permute-start.4) | collective-permute-done | bytes 262176 | tf_op jit(solution)/shard_map/ppermute | solution.py:32
  53.3 0.7 %shard_map.81 = (bf16[256,256]{1,0:T(8,128)(2,1)}, bf16[256,256]{1,0:T(8,128)(2,1)}) custom-call(f32[2,256,256]{2,1,0:T(8,128)S(1)} %get-tuple-element.32.sum_ref, bf16[2,256,256]{2,1,0:T(8,128)(2,1)S(1)} %collective-permute-done.4.n2), custom_call_target="tpu_custom_call" | custom-call | bytes 1048576 | tf_op jit(solution)/shard_map/pallas_call | solution.py:300
Async XLA Ops:
  3.1 19.1 %all-to-all-start = ((bf16[4,2,256,256]{3,2,1,0:T(8,128)(2,1)}), bf16[4,2,256,256]{3,2,1,0:T(8,128)(2,1)S(1)}, u32[]{:S(2)}, u32[]{:S(2)}) async-start(bf16[4,2,256,256]{3,2,1,0:T(8,128)(2,1)} %get-tuple-element.21), calls=%async_computation | async-start | bytes 2097152 | tf_op jit(solution)/shard_map/all_to_all | solution.py:269
  8.0 12.2 %collective-permute-start = (bf16[2,256,256]{2,1,0:T(8,128)(2,1)S(1)}, bf16[2,256,256]{2,1,0:T(8,128)(2,1)S(1)}, u32[]{:S(2)}, u32[]{:S(2)}) collective-permute-start(bf16[2,256,256]{2,1,0:T(8,128)(2,1)S(1)} %get-tuple-element.22.refs_2_), channel_id=1, source_target_pairs={{0,8},{4,12},{8,16},{12,20},{16,24},{20,28},{24,32},{28,36},{32,40... | collective-permute-start | bytes 786440 | tf_op jit(solution)/shard_map/ppermute | solution.py:32
  13.0 9.2 %collective-permute-start.1 = (bf16[2,256,256]{2,1,0:T(8,128)(2,1)S(1)}, bf16[2,256,256]{2,1,0:T(8,128)(2,1)S(1)}, u32[]{:S(2)}, u32[]{:S(2)}) collective-permute-start(bf16[2,256,256]{2,1,0:T(8,128)(2,1)S(1)} %get-tuple-element.22.refs_2_), channel_id=1, source_target_pairs={{0,4},{4,16},{8,12},{12,24},{16,20},{20,32},{24,28},{28,40},{32,36... | collective-permute-start | bytes 786440 | tf_op jit(solution)/shard_map/ppermute | solution.py:32
  20.2 4.3 %collective-permute-start.2 = (bf16[2,256,256]{2,1,0:T(8,128)(2,1)S(1)}, bf16[2,256,256]{2,1,0:T(8,128)(2,1)S(1)}, u32[]{:S(2)}, u32[]{:S(2)}) collective-permute-start(bf16[2,256,256]{2,1,0:T(8,128)(2,1)S(1)} %collective-permute-done.refs_0_), channel_id=1, source_target_pairs={{0,4},{4,0},{8,12},{12,8},{16,20},{20,16},{24,28},{28,24},{32,36},... | collective-permute-start | bytes 786440 | tf_op jit(solution)/shard_map/ppermute | solution.py:32
  30.4 13.5 %all-to-all-start.1 = ((bf16[4,256,256]{2,1,0:T(8,128)(2,1)}), bf16[4,256,256]{2,1,0:T(8,128)(2,1)S(1)}, u32[]{:S(2)}, u32[]{:S(2)}) async-start(bf16[4,256,256]{2,1,0:T(8,128)(2,1)} %get-tuple-element.30), calls=%async_computation.1 | async-start | bytes 1048576 | tf_op jit(solution)/shard_map/all_to_all | solution.py:296
  35.2 7.1 %collective-permute-start.3 = (bf16[2,256,256]{2,1,0:T(8,128)(2,1)S(1)}, bf16[2,256,256]{2,1,0:T(8,128)(2,1)S(1)}, u32[]{:S(2)}, u32[]{:S(2)}) collective-permute-start(bf16[2,256,256]{2,1,0:T(8,128)(2,1)S(1)} %get-tuple-element.29), channel_id=1, source_target_pairs={{4,0},{12,8},{16,4},{20,16},{24,12},{28,24},{32,20},{36,32},{40,28... | collective-permute-start | bytes 786440 | tf_op jit(solution)/shard_map/ppermute | solution.py:32
  39.5 13.8 %collective-permute-start.4 = (bf16[2,256,256]{2,1,0:T(8,128)(2,1)S(1)}, bf16[2,256,256]{2,1,0:T(8,128)(2,1)S(1)}, u32[]{:S(2)}, u32[]{:S(2)}) collective-permute-start(bf16[2,256,256]{2,1,0:T(8,128)(2,1)S(1)} %shard_map.80), channel_id=1, source_target_pairs={{8,0},{12,4},{16,8},{20,12},{24,16},{28,20},{32,24},{36,28},{40,32... | collective-permute-start | bytes 786440 | tf_op jit(solution)/shard_map/ppermute | solution.py:32
